TPU v7x, 512 devices: a whole 4x8x8 slice. The times are simulated.
512 devices in a mesh: gx: 32 (over y, z_lo, core), gy: 16 (over x, z_hi).
Axes of the slice: x: 4, y: 8, z: 8 (z_hi: 4, z_lo: 2; z = z_hi * 2 + z_lo), core: 2. Of those that a mesh axis runs over, the one named last changes fastest.
Arguments:
- field: bfloat16 [512, 256, 4, 64], P('gx', 'gy'), may hold values from -6 to 6
- first_kernel: bfloat16 [1728, 64], replicated, may hold values from -0.21875 to 0.21875
- second_kernel: bfloat16 [1728, 64], replicated, may hold values from -0.15625 to 0.15625
- cotangent: bfloat16 [512, 256, 4, 64], P('gx', 'gy'), may hold values from -6 to 6
- samples: int32 [32, 16, 256], P('gx', 'gy'), may hold values from 0 to 1023
Outputs:
- output: bfloat16 [512, 256, 4, 64], P('gx', 'gy')
- first_update: float32 [1728, 64], replicated
- second_update: float32 [1728, 64], replicated
All inputs are finite; a program needn't handle non-finite values.
Results may differ from a plain program's by a relative error of at most 0.0034.
Values may be sent and summed in bfloat16 or wider, within the bound.
A program may use at most 64 MiB of HBM per device.

v0:
```python
import jax
import jax.numpy as jnp
from jax import lax
from jax.sharding import PartitionSpec as P

NS_ITERS = 5


def with_halo(block, sides, width):
    for axis, dim in sides:
        count = lax.axis_size(axis)
        forward = [(i, i + 1) for i in range(count - 1)]
        backward = [(target, source) for source, target in forward]
        low = lax.ppermute(
            lax.slice_in_dim(block, block.shape[dim] - width, None, axis=dim), axis, forward
        )
        high = lax.ppermute(lax.slice_in_dim(block, 0, width, axis=dim), axis, backward)
        block = jnp.concatenate([low, block, high], axis=dim)
    return block


def patches(padded, row_index, ylen, zlen):
    slab = lax.dynamic_slice_in_dim(padded, row_index, 3, 0)
    pieces = [
        slab[first, second : second + ylen, third : third + zlen, :]
        for first in range(3)
        for second in range(3)
        for third in range(3)
    ]
    return jnp.concatenate(pieces, -1).reshape(ylen * zlen, -1)


def convolve(framed, kernel):
    padded = jnp.pad(framed, ((0, 0), (0, 0), (1, 1), (0, 0)))
    xlen = framed.shape[0] - 2
    ylen = framed.shape[1] - 2
    zlen = framed.shape[2]
    width = kernel.shape[1]

    def one_row(row_index):
        return jnp.dot(
            patches(padded, row_index, ylen, zlen), kernel, preferred_element_type=jnp.float32
        )

    result = lax.map(one_row, jnp.arange(xlen, dtype=jnp.int32))
    return result.reshape(xlen, ylen, zlen, width)


def kernel_grad(framed, grads):
    padded = jnp.pad(framed, ((0, 0), (0, 0), (1, 1), (0, 0)))
    xlen, ylen, zlen, width = grads.shape

    def add_row(row_index, total):
        block = lax.dynamic_index_in_dim(grads, row_index, 0, keepdims=False).reshape(
            ylen * zlen, width
        )
        return total + jnp.dot(
            patches(padded, row_index, ylen, zlen).T, block, preferred_element_type=jnp.float32
        )

    start = jnp.zeros((27 * framed.shape[3], width), jnp.float32)
    return lax.fori_loop(0, xlen, add_row, start)


def flip_kernel(kernel, width):
    blocks = kernel.reshape(3, 3, 3, width, width)[::-1, ::-1, ::-1]
    return jnp.transpose(blocks, (0, 1, 2, 4, 3)).reshape(27 * width, width)


def newton_inverse(factor):
    width = factor.shape[0]
    identity = jnp.eye(width, dtype=jnp.float32)
    matrix = factor + 0.1 * identity
    approx = identity / jnp.sqrt(jnp.sum(matrix * matrix))
    for step in range(NS_ITERS):
        inner = 2.0 * identity - jnp.dot(matrix, approx, precision=lax.Precision.HIGHEST)
        approx = jnp.dot(approx, inner, precision=lax.Precision.HIGHEST)
    return approx


def precondition(grad, left_inv, right_inv, width):
    blocks = grad.reshape(27, width, width)
    result = jnp.einsum(
        "ab,tbc,cd->tad", left_inv, blocks, right_inv, precision=lax.Precision.HIGHEST
    )
    return result.reshape(27 * width, width)


def local_gram(values, cells, count):
    width = values.shape[3]
    picked = jnp.take(values.reshape(-1, width), cells, axis=0)
    return jnp.dot(picked.T, picked, preferred_element_type=jnp.float32) / count


def layer_inverses(inputs, outputs, cells, count):
    left_gram, right_gram = lax.psum(
        (local_gram(inputs, cells, count), local_gram(outputs, cells, count)), ("gx", "gy")
    )
    return (newton_inverse(left_gram), newton_inverse(right_gram))


def local(field, first_kernel, second_kernel, cotangent, samples):
    width = field.shape[3]
    xlen, ylen, zlen = (field.shape[0], field.shape[1], field.shape[2])
    tiles = lax.axis_size("gx") * lax.axis_size("gy")
    count = jnp.float32(tiles * samples.shape[2])
    cells = samples.reshape(-1)
    scale = 1.0 / jnp.sqrt(jnp.float32(tiles * xlen * ylen * zlen))
    framed_field = with_halo(field, (("gx", 0), ("gy", 1)), 1)
    hidden_pre = convolve(framed_field, first_kernel)
    hidden = jax.nn.silu(hidden_pre).astype(jnp.bfloat16)
    framed_hidden = with_halo(hidden, (("gx", 0), ("gy", 1)), 1)
    output = (field.astype(jnp.float32) + convolve(framed_hidden, second_kernel)).astype(
        jnp.bfloat16
    )
    framed_cotangent = with_halo(cotangent, (("gx", 0), ("gy", 1)), 1)
    second_grad = kernel_grad(framed_hidden, cotangent) * scale
    second_left, second_right = layer_inverses(hidden, cotangent, cells, count)
    back = convolve(framed_cotangent, flip_kernel(second_kernel, width))
    sigma = jax.nn.sigmoid(hidden_pre)
    delta = (back * sigma * (1.0 + hidden_pre * (1.0 - sigma))).astype(jnp.bfloat16)
    first_grad = kernel_grad(framed_field, delta) * scale
    first_left, first_right = layer_inverses(field, delta, cells, count)
    second_total, first_total = lax.psum((second_grad, first_grad), ("gx", "gy"))
    first_update = precondition(first_total, first_left, first_right, width)
    second_update = precondition(second_total, second_left, second_right, width)
    return (output, first_update, second_update)


def solution(mesh):
    placed = (P("gx", "gy", None, None), P(), P(), P("gx", "gy", None, None), P("gx", "gy", None))
    return jax.shard_map(
        local,
        mesh=mesh,
        in_specs=placed,
        out_specs=(P("gx", "gy", None, None), P(), P()),
        check_vma=False,
    )
```

profile of v0, /device:TPU:1, one launch (start us, length us, event | category | flops | bytes accessed | tf_op | source)
XLA Modules:
  0.0 836.5 jit_solution(13182387417172492346)
XLA Ops:
  8.0 5.4 collective-permute-start
  13.4 4.7 collective-permute-start.1
  18.9 1.9 collective-permute-start.8
  20.8 2.4 collective-permute-start.9
  24.6 1.7 gather_fusion.3
  29.3 1.7 rev.3
  31.4 4.3 collective-permute-start.2
  35.7 1.3 collective-permute-start.3
  37.9 7.3 collective-permute-start.10
  45.2 1.3 collective-permute-start.11
  47.0 75.0 %while.58 = (s32[]{:T(128)}, f32[16,64,64]{2,1,0:T(8,128)S(1)}, s32[16]{0:T(128)S(1)}, bf16[18,18,6,64]{3,2,1,0:T(8,128)(2,1)S(1)}, bf16[1728,64]{0,1:T(8,128)(2...) while((s32[]{:T(128)}, f32[16,64,64]{2,1,0:T(8,128)S(1)}, s32[16]{0:T(128)S(1)}, ...), condition=%wide.region_1.2_spmd, body=%wide.region_0.1_spmd.sunk | while | flops 14155785 | bytes 1376475 | solution.py:45
  122.0 1.5 select_maximum_fusion
  125.0 96.4 %while.60 = (s32[]{:T(128)}, f32[16,64,64]{2,1,0:T(8,128)}, s32[16]{0:T(128)}, bf16[18,18,6,64]{3,2,1,0:T(8,128)(2,1)S(1)}, bf16[1728,64]{1,0:T(8,128)(2,1)S(1)}...) while((s32[]{:T(128)}, f32[16,64,64]{2,1,0:T(8,128)}, s32[16]{0:T(128)}, ...), condition=%wide.region_5.6_spmd, body=%wide.region_4.5_spmd.sunk | while | flops 14155785 | bytes 1360599 | solution.py:45
  125.0 1.2 dynamic_slice.59
  129.1 1.1 concatenate.385
  131.0 1.2 dynamic_slice.59
  135.1 1.1 concatenate.385
  137.0 1.2 dynamic_slice.59
  143.1 1.2 dynamic_slice.59
  149.1 1.2 dynamic_slice.59
  155.1 1.2 dynamic_slice.59
  161.1 1.2 dynamic_slice.59
  167.2 1.2 dynamic_slice.59
  173.2 1.2 dynamic_slice.59
  179.2 1.2 dynamic_slice.59
  185.2 1.2 dynamic_slice.59
  191.3 1.2 dynamic_slice.59
  197.3 1.2 dynamic_slice.59
  203.3 1.2 dynamic_slice.59
  209.3 1.2 dynamic_slice.59
  215.3 1.2 dynamic_slice.59
  221.4 1.5 fusion.20
  223.8 1.2 multiply_convert_fusion
  225.0 4.2 collective-permute-start.4
  229.2 1.9 collective-permute-start.5
  231.2 25.0 %while.61 = (s32[]{:T(128)}, f32[1728,64]{0,1:T(8,128)S(1)}, bf16[18,18,6,64]{3,2,1,0:T(8,128)(2,1)S(1)}, bf16[16,16,4,64]{3,2,1,0:T(4,128)(2,1)}, s32[]{:T(128)}, /*index=5*/s32[]{}, s32[]{:T(128)}, s32[]{}) while((s32[]{:T(128)}, f32[1728,64]{0,1:T(8,128)S(1)}, bf16[18,18,6,64]{3,2,1,0:T(8,128)(2,1)S(1)}, ...), condition=%wide.region_7.8_spmd.clone, body=%wide.region_6.7_spmd.clone.sunk | while | flops 14376967 | bytes 2015395 | solution.py:62
  258.0 5.8 collective-permute-start.6
  263.8 1.3 collective-permute-start.7
  266.4 1.5 copy.15
  268.1 2.6 collective-permute-done.7
  271.2 25.0 %while.62 = (s32[]{:T(128)}, f32[1728,64]{0,1:T(8,128)S(1)}, bf16[18,18,6,64]{3,2,1,0:T(8,128)(2,1)S(1)}, bf16[16,16,4,64]{3,2,1,0:T(4,128)(2,1)}, s32[]{:T(128)}, /*index=5*/s32[]{}, s32[]{:T(128)}, s32[]{}) while((s32[]{:T(128)}, f32[1728,64]{0,1:T(8,128)S(1)}, bf16[18,18,6,64]{3,2,1,0:T(8,128)(2,1)S(1)}, ...), condition=%wide.region_14.16_spmd.clone, body=%wide.region_13.15_spmd.clone.sunk | while | flops 14376967 | bytes 2015395 | solution.py:62
  296.4 51.7 %while.59 = (s32[]{:T(128)}, f32[16,64,64]{2,1,0:T(8,128)S(1)}, s32[16]{0:T(128)S(1)}, bf16[18,18,6,64]{3,2,1,0:T(8,128)(2,1)S(1)}, bf16[1728,64]{0,1:T(8,128)(2...) while((s32[]{:T(128)}, f32[16,64,64]{2,1,0:T(8,128)S(1)}, s32[16]{0:T(128)S(1)}, ...), condition=%wide.region_3.4_spmd, body=%wide.region_2.3_spmd.sunk | while | flops 14155785 | bytes 1376475 | solution.py:45
  349.4 1.5 copy.17
  350.9 191.8 %all-reduce.8.cloned.1.call-done = (f32[64,64]{1,0:T(8,128)}, f32[64,64]{1,0:T(8,128)}, f32[64,64]{1,0:T(8,128)}, f32[64,64]{1,0:T(8,128)}) async-done(((f32[64,64]{1,0:T(8,128)}, f32[64,64]{1,0:T(8,128)}, f32[64,64]{1,0:T(8,128)}, f32[64,64]{1,0:T(8,128)}), (f32[64,64]{1,0:T(8,128)}, f32[64,64]{1,0:T(8,128)}, f32[64,64]{1,0:T(8,128)}, f32[64,64]{1,0:T(8,128)})) %all-reduce.8.cloned.1.call-update) | async-done | bytes 65552 | tf_op jit(solution)/shard_map/psum | solution.py:96
  542.6 1.4 multiply_reduce_fusion
  558.8 261.0 %all-reduce.10.cloned.1.call-done = (f32[27,64,64]{1,2,0:T(8,128)}, f32[27,64,64]{1,2,0:T(8,128)}) async-done(((f32[27,64,64]{1,2,0:T(8,128)}, f32[27,64,64]{1,2,0:T(8,128)}), (f32[27,64,64]{1,2,0:T(8,128)}, f32[27,64,64]{1,2,0:T(8,128)})) %all-reduce.10.cloned.1.call-update) | async-done | bytes 884752 | tf_op jit(solution)/shard_map/psum | solution.py:124
  819.9 3.5 fusion.125
  825.4 2.4 fusion.117
  (403 shorter events, 186.6 us)
Async XLA Ops:
  7.2 19.2 %copy-start.5 = (bf16[16,16,4,64]{3,2,1,0:T(4,128)(2,1)S(1)}, bf16[16,16,4,64]{3,2,1,0:T(4,128)(2,1)}, u32[]{:S(2)}) copy-start(bf16[16,16,4,64]{3,2,1,0:T(4,128)(2,1)} %param.17) | copy-start | bytes 393220
  7.2 21.8 %copy-start = (bf16[1728,64]{0,1:T(8,128)(2,1)S(1)}, bf16[1728,64]{0,1:T(8,128)(2,1)}, u32[]{:S(2)}) copy-start(bf16[1728,64]{0,1:T(8,128)(2,1)} %param.19) | copy-start | bytes 663556
  7.2 535.5 %all-reduce.8.cloned.1.call-start = ((), (), s32[]{:S(2)}) async-start(), calls=%async_computation | async-start | bytes 262144 | tf_op jit(solution)/shard_map/psum | solution.py:96
  8.0 23.1 %collective-permute-start = (bf16[1,16,4,64]{3,2,1,0:T(4,128)(2,1)S(1)}, bf16[1,16,4,64]{3,2,1,0:T(4,128)(2,1)S(1)}, u32[]{:S(2)}, u32[]{:S(2)}) collective-permute-start(bf16[1,16,4,64]{3,2,1,0:T(4,128)(2,1)S(1)} %get-tuple-element.496), channel_id=1, source_target_pairs={{0,16},{16,32},{32,48},{48,64},{64,80},{80,96},{96,112},{112,128},... | collective-permute-start | bytes 24584 | tf_op jit(solution)/shard_map/ppermute | solution.py:14
  13.4 17.9 %collective-permute-start.1 = (bf16[1,16,4,64]{3,2,1,0:T(4,128)(2,1)S(1)}, bf16[1,16,4,64]{3,2,1,0:T(4,128)(2,1)S(1)}, u32[]{:S(2)}, u32[]{:S(2)}) collective-permute-start(bf16[1,16,4,64]{3,2,1,0:T(4,128)(2,1)S(1)} %get-tuple-element.495), channel_id=1, source_target_pairs={{16,0},{32,16},{48,32},{64,48},{80,64},{96,80},{112,96},{128,112},... | collective-permute-start | bytes 24584 | tf_op jit(solution)/shard_map/ppermute | solution.py:17
  18.9 18.1 %collective-permute-start.8 = (bf16[1,16,4,64]{3,2,1,0:T(4,128)(2,1)S(1)}, bf16[1,16,4,64]{3,2,1,0:T(4,128)(2,1)S(1)}, u32[]{:S(2)}, u32[]{:S(2)}) collective-permute-start(bf16[1,16,4,64]{3,2,1,0:T(4,128)(2,1)S(1)} %get-tuple-element.492), channel_id=1, source_target_pairs={{0,16},{16,32},{32,48},{48,64},{64,80},{80,96},{96,112},{112,128},... | collective-permute-start | bytes 24584 | tf_op jit(solution)/shard_map/ppermute | solution.py:14
  20.8 16.3 %collective-permute-start.9 = (bf16[1,16,4,64]{3,2,1,0:T(4,128)(2,1)S(1)}, bf16[1,16,4,64]{3,2,1,0:T(4,128)(2,1)S(1)}, u32[]{:S(2)}, u32[]{:S(2)}) collective-permute-start(bf16[1,16,4,64]{3,2,1,0:T(4,128)(2,1)S(1)} %get-tuple-element.491), channel_id=1, source_target_pairs={{16,0},{32,16},{48,32},{64,48},{80,64},{96,80},{112,96},{128,112},... | collective-permute-start | bytes 24584 | tf_op jit(solution)/shard_map/ppermute | solution.py:17
  24.6 4.7 copy-start.15
  24.6 4.4 copy-start.13
  31.0 6.0 copy-start.7
  31.4 15.1 %collective-permute-start.2 = (bf16[18,1,4,64]{3,2,1,0:T(4,128)(2,1)S(1)}, bf16[18,1,4,64]{3,2,1,0:T(4,128)(2,1)S(1)}, u32[]{:S(2)}, u32[]{:S(2)}) collective-permute-start(bf16[18,1,4,64]{3,2,1,0:T(4,128)(2,1)S(1)} %get-tuple-element.489), channel_id=1, source_target_pairs={{0,1},{1,2},{2,3},{3,4},{4,5},{5,6},{6,7},{7,8},{8,9},{9,10},{10,1... | collective-permute-start | bytes 27656 | tf_op jit(solution)/shard_map/ppermute | solution.py:14
  35.7 10.9 %collective-permute-start.3 = (bf16[18,1,4,64]{3,2,1,0:T(4,128)(2,1)S(1)}, bf16[18,1,4,64]{3,2,1,0:T(4,128)(2,1)S(1)}, u32[]{:S(2)}, u32[]{:S(2)}) collective-permute-start(bf16[18,1,4,64]{3,2,1,0:T(4,128)(2,1)S(1)} %get-tuple-element.490), channel_id=1, source_target_pairs={{1,0},{2,1},{3,2},{4,3},{5,4},{6,5},{7,6},{8,7},{9,8},{10,9},{11,1... | collective-permute-start | bytes 27656 | tf_op jit(solution)/shard_map/ppermute | solution.py:17
  37.0 10.0 %copy-start.1 = (bf16[1728,64]{0,1:T(8,128)(2,1)S(1)}, bf16[1728,64]{0,1:T(8,128)(2,1)}, u32[]{:S(2)}) copy-start(bf16[1728,64]{0,1:T(8,128)(2,1)} %param.18) | copy-start | bytes 663556
  37.2 9.7 %copy-start.12 = (bf16[18,16,4,64]{3,2,1,0:T(4,128)(2,1)}, bf16[18,16,4,64]{3,2,1,0:T(4,128)(2,1)S(1)}, u32[]{:S(2)}) copy-start(bf16[18,16,4,64]{3,2,1,0:T(4,128)(2,1)S(1)} %constant_dynamic-update-slice_fusion.3) | copy-start | bytes 442372
  37.9 84.1 %collective-permute-start.10 = (bf16[18,1,4,64]{3,2,1,0:T(4,128)(2,1)}, bf16[18,1,4,64]{3,2,1,0:T(4,128)(2,1)}, u32[]{:S(2)}, u32[]{:S(2)}) collective-permute-start(bf16[18,1,4,64]{3,2,1,0:T(4,128)(2,1)} %get-tuple-element.485), channel_id=1, source_target_pairs={{0,1},{1,2},{2,3},{3,4},{4,5},{5,6},{6,7},{7,8},{8,9},{9,10},{10,1... | collective-permute-start | bytes 27656 | tf_op jit(solution)/shard_map/ppermute | solution.py:14
  45.2 76.8 %collective-permute-start.11 = (bf16[18,1,4,64]{3,2,1,0:T(4,128)(2,1)}, bf16[18,1,4,64]{3,2,1,0:T(4,128)(2,1)}, u32[]{:S(2)}, u32[]{:S(2)}) collective-permute-start(bf16[18,1,4,64]{3,2,1,0:T(4,128)(2,1)} %get-tuple-element.486), channel_id=1, source_target_pairs={{1,0},{2,1},{3,2},{4,3},{5,4},{6,5},{7,6},{8,7},{9,8},{10,9},{11,1... | collective-permute-start | bytes 27656 | tf_op jit(solution)/shard_map/ppermute | solution.py:17
  122.0 3.0 copy-start.2
  221.4 1.6 copy-start.14
  221.4 2.4 copy-start.3
  221.4 2.4 copy-start.4
  225.0 33.0 %collective-permute-start.4 = (bf16[1,16,4,64]{3,2,1,0:T(4,128)(2,1)S(1)}, bf16[1,16,4,64]{3,2,1,0:T(4,128)(2,1)S(1)}, u32[]{:S(2)}, u32[]{:S(2)}) collective-permute-start(bf16[1,16,4,64]{3,2,1,0:T(4,128)(2,1)S(1)} %get-tuple-element.493), channel_id=1, source_target_pairs={{0,16},{16,32},{32,48},{48,64},{64,80},{80,96},{96,112},{112,128},... | collective-permute-start | bytes 24584 | tf_op jit(solution)/shard_map/ppermute | solution.py:14
  229.2 28.8 %collective-permute-start.5 = (bf16[1,16,4,64]{3,2,1,0:T(4,128)(2,1)S(1)}, bf16[1,16,4,64]{3,2,1,0:T(4,128)(2,1)S(1)}, u32[]{:S(2)}, u32[]{:S(2)}) collective-permute-start(bf16[1,16,4,64]{3,2,1,0:T(4,128)(2,1)S(1)} %get-tuple-element.494), channel_id=1, source_target_pairs={{16,0},{32,16},{48,32},{64,48},{80,64},{96,80},{112,96},{128,112},... | collective-permute-start | bytes 24584 | tf_op jit(solution)/shard_map/ppermute | solution.py:17
  231.1 25.1 %copy-start.16 = (pred[256]{0:T(512)(128)(4,1)S(1)}, pred[256]{0:T(512)(128)(4,1)}, u32[]{:S(2)}) copy-start(pred[256]{0:T(512)(128)(4,1)} %copy-done.15) | copy-start | bytes 772
  258.0 10.1 %collective-permute-start.6 = (bf16[18,1,4,64]{3,2,1,0:T(4,128)(2,1)S(1)}, bf16[18,1,4,64]{3,2,1,0:T(4,128)(2,1)S(1)}, u32[]{:S(2)}, u32[]{:S(2)}) collective-permute-start(bf16[18,1,4,64]{3,2,1,0:T(4,128)(2,1)S(1)} %get-tuple-element.487), channel_id=1, source_target_pairs={{0,1},{1,2},{2,3},{3,4},{4,5},{5,6},{6,7},{7,8},{8,9},{9,10},{10,1... | collective-permute-start | bytes 27656 | tf_op jit(solution)/shard_map/ppermute | solution.py:14
  263.8 6.9 collective-permute-start.7
  267.9 552.0 %all-reduce.10.cloned.1.call-start = ((), (), s32[]{:S(2)}) async-start(), calls=%async_computation.1 | async-start | bytes 3538944 | tf_op jit(solution)/shard_map/psum | solution.py:124
  296.3 51.8 %copy-start.6 = (bf16[16,16,4,64]{3,2,1,0:T(4,128)(2,1)S(1)}, bf16[16,16,4,64]{3,2,1,0:T(4,128)(2,1)}, u32[]{:S(2)}) copy-start(bf16[16,16,4,64]{3,2,1,0:T(4,128)(2,1)} %param.17) | copy-start | bytes 393220
  542.6 9.4 %copy-start.11 = (f32[64,64]{1,0:T(8,128)S(1)}, f32[64,64]{1,0:T(8,128)}, u32[]{:S(2)}) copy-start(f32[64,64]{1,0:T(8,128)} %get-tuple-element.340) | copy-start | bytes 49156
  542.6 10.8 %copy-start.9 = (f32[64,64]{1,0:T(8,128)S(1)}, f32[64,64]{1,0:T(8,128)}, u32[]{:S(2)}) copy-start(f32[64,64]{1,0:T(8,128)} %get-tuple-element.338) | copy-start | bytes 49156
  542.6 10.8 %copy-start.10 = (f32[64,64]{1,0:T(8,128)S(1)}, f32[64,64]{1,0:T(8,128)}, u32[]{:S(2)}) copy-start(f32[64,64]{1,0:T(8,128)} %get-tuple-element.339) | copy-start | bytes 49156
  824.3 1.2 copy-start.8
Sparse Core Ops, SparseCore 0:
  268.0 274.5 all-reduce.7
  548.5 271.3 all-reduce.9
where the time goes:
time: 845 us; the launch traced here: 837 us
  waiting for transfers between devices  455 us (54%)
  local copies, waits for them, and re-layouts  165 us (20%)
  loops' own time  95.5 us (11%)
  matrix products  51.6 us (6%)
  starting transfers between devices  42.1 us (5%)
  between operations  17.7 us (2%)
  other arithmetic  9.56 us (1%)
    psum x1, waiting for transfers between devices, local(): lax.psum((second_grad, first_grad), ('gx', 'gy'))  261 us
    psum x1, waiting for transfers between devices, layer_inverses(): lax.psum((local_gram(inputs, cells, count), local_gram(outputs, cells, co...  192 us
    another operation x3, loops' own time, convolve(): result = lax.map(one_row, jnp.arange(xlen, dtype=jnp.int32))  94.1 us
    slice x80, local copies, waits for them, and re-layouts, patches(): slab[first, second:second + ylen, third:third + zlen, :]  68.1 us
    concatenate x80, local copies, waits for them, and re-layouts, patches(): return jnp.concatenate(pieces, -1).reshape(ylen * zlen, -1)  41.4 us
    dynamic_slice x48, local copies, waits for them, and re-layouts, convolve(): result = lax.map(one_row, jnp.arange(xlen, dtype=jnp.int32))  38.6 us
    ppermute x6, starting transfers between devices, with_halo(): lax.ppermute(lax.slice_in_dim(block, block.shape[dim] - width, None, axis...  28.9 us
    dot_general x48, matrix products, one_row(): jnp.dot(patches(padded, row_index, ylen, zlen), kernel, preferred_element...  19.9 us
  transfers between devices with their start and end apart: 14, of which 3 were waited for; matrix products, arithmetic and copies ran while one was open for 17% of the time, Pallas kernels for 0%

commit v1 on v0

v1 whole, which is shorter than its diff:
```python
import functools

import jax
import jax.numpy as jnp
from jax import lax
from jax.experimental import pallas as pl
from jax.experimental.pallas import tpu as pltpu
from jax.sharding import PartitionSpec as P

MESH = pl.DeviceIdType.MESH
F32 = jnp.float32
BF16 = jnp.bfloat16
NS_ITERS = 5
C = 64
TX = 16
TY = 16
NZ = 4
WIDE = NZ * C
CELLS = TX * TY
BLOCKS = 32
HALF = BLOCKS * 64 // 2
FIELD, COT, HIDDEN = 0, 1, 2
NN = (((1,), (0,)), ((), ()))
NT = (((1,), (1,)), ((), ()))


def dot(a, b, dims=NN):
    return lax.dot_general(a, b, dims, preferred_element_type=F32)


def dot32(a, b, dims=NN):
    return lax.dot_general(a, b, dims, precision=lax.Precision.HIGHEST, preferred_element_type=F32)


def iota(shape, dim):
    return lax.broadcasted_iota(jnp.int32, shape, dim)


def onehot(target, shape):
    return jnp.where(iota(shape, 1) == target, 1.0, 0.0).astype(BF16)


def swap_halves(value):
    return pltpu.roll(value, 64, 1)


def kernel(
    sizes,
    field_ref,
    first_ref,
    second_ref,
    cot_ref,
    samples_ref,
    out_ref,
    first_out,
    second_out,
    src,
    col,
    cat,
    band,
    grads,
    pay,
    core_in,
    axis_in,
    plane_out,
    plane_in,
    full,
    metric,
    halo_send,
    halo_recv,
    core_send,
    core_recv,
    axis_send,
    axis_recv,
    plane_send,
    plane_recv,
    gather_send,
    gather_recv,
    spread_send,
    spread_recv,
    back_send,
    back_recv,
):
    n_gx, n_gy, z_hi, ring, plane, part = sizes
    gx = lax.axis_index("gx")
    gy = lax.axis_index("gy")
    core = lax.rem(gx, 2)
    z_low = lax.rem(lax.div(gx, 2), 2)
    y = lax.div(gx, 4)
    x = lax.div(gy, z_hi)
    z = lax.rem(gy, z_hi) * 2 + z_low

    def device(px, py, pz, pcore):
        return ((py * 2 + lax.rem(pz, 2)) * 2 + pcore, px * z_hi + lax.div(pz, 2))

    rank = y + core * (z - y)
    spot = x * ring + z + core * (y - z)
    group = lax.div(spot, part)
    slot = lax.rem(spot, part)
    partner = device(x, y, z, 1 - core)

    def on_ring(j):
        return device(x, y + (1 - core) * (j - y), z + core * (j - z), core)

    def on_plane(j):
        px, w = lax.div(j, ring), lax.rem(j, ring)
        return device(px, y + core * (w - y), z + (1 - core) * (w - z), core)

    def neighbour(dx, dy):
        return (lax.rem(gx + n_gx + dx, n_gx), lax.rem(gy + n_gy + dy, n_gy))

    def signal(where):
        pl.semaphore_signal(barrier, inc=1, device_id=where, device_id_type=MESH)

    barrier = pltpu.get_barrier_semaphore()
    sides = ((1, 0), (-1, 0), (0, 1), (0, -1), (1, 1), (1, -1), (-1, 1), (-1, -1))
    for side in sides:
        signal(neighbour(*side))
    signal(partner)

    @pl.loop(1, ring)
    def _(k):
        signal(on_ring(lax.rem(rank + k, ring)))

    @pl.loop(1, plane)
    def _(k):
        signal(on_plane(lax.rem(spot + k, plane)))

    def copy(source, target, send, recv, where):
        return pltpu.make_async_remote_copy(
            src_ref=source,
            dst_ref=target,
            send_sem=send,
            recv_sem=recv,
            device_id=where,
            device_id_type=MESH,
        )

    def halo(a, d):
        side = sides[d]
        if side[0] == 0:
            source = col.at[a, 1 if side[1] > 0 else 0]
        else:
            source = src.at[a, TX if side[0] > 0 else 1]
        landing = (0, TX + 1, TX + 2, TX + 3, TX + 4, TX + 5, TX + 6, TX + 7)[d]
        return copy(
            source, src.at[a, landing], halo_send.at[a, d], halo_recv.at[a, d], neighbour(*side)
        )

    edge_rows = iota((2 * TX, 1), 0)
    edges = onehot(jnp.where(edge_rows < TX, edge_rows * TY, (edge_rows - TX) * TY + TY - 1), (2 * TX, CELLS))

    def keep(a, value):
        src[a, 1 : TX + 1] = value.reshape(TX, TY, WIDE)
        col[a] = dot(edges, value).astype(BF16).reshape(2, TX, WIDE)

    rows256 = iota((256, 1), 0)
    to_columns = onehot(lax.rem(rows256, 64) * NZ + lax.div(rows256, 64), (256, 256))
    to_cells = onehot(lax.rem(rows256, NZ) * 64 + lax.div(rows256, NZ), (256, 256))

    def columns_of(ref):
        out = []
        for b in range(4):
            moved = dot(to_columns, ref[b * 256 : (b + 1) * 256, :])
            out.append(jnp.concatenate([moved[i * 64 : (i + 1) * 64] for i in range(NZ)], axis=1))
        return jnp.concatenate(out, axis=0).astype(BF16)

    keep(FIELD, columns_of(field_ref))
    keep(COT, columns_of(cot_ref))

    pl.semaphore_wait(barrier, len(sides) + 1 + (ring - 1) + (plane - 1))
    for a in (FIELD, COT):
        for d in range(8):
            halo(a, d).start()

    def build_band(layer, ref):
        nothing = jnp.zeros((64, 64), F32)
        for k in range(9):
            low, mid, high = (
                ref[:, (3 * k + i) * 64 : (3 * k + i + 1) * 64].astype(F32) for i in range(3)
            )
            lanes = slice((k % 3) * WIDE, (k % 3 + 1) * WIDE)
            for out_z, parts in enumerate(
                (
                    (mid, high, nothing, nothing),
                    (low, mid, high, nothing),
                    (nothing, low, mid, high),
                    (nothing, nothing, low, mid),
                )
            ):
                band[layer, k // 3, out_z * 64 : (out_z + 1) * 64, lanes] = jnp.concatenate(
                    parts, axis=1
                ).astype(BF16)

    build_band(0, first_ref)
    build_band(1, second_ref)

    framed_rows = (TX + 2) * TY
    source_rows = (TX + 8) * TY
    i = iota((framed_rows, 1), 0)
    r = lax.div(i, TY)
    c = lax.rem(i, TY)
    first_row, last_row = jnp.where(gx == 0, 0, -1), jnp.where(gx == n_gx - 1, TX + 1, -1)
    first_col, last_col = jnp.where(gy == 0, 0, -1), jnp.where(gy == n_gy - 1, TY - 1, -1)
    outside = (r == first_row) | (r == last_row)

    def shifted(step, at, column_slot, low_slot, high_slot, pick, outer):
        edge = jnp.where(
            r == 0,
            low_slot * TY + pick,
            jnp.where(r == TX + 1, high_slot * TY + pick, column_slot * TY + r - 1),
        )
        target = jnp.where(c == at, edge, i + step)
        return onehot(jnp.where(outside | (c == outer), -1, target), (framed_rows, source_rows))

    shift_low = shifted(-1, 0, TX + 2, TX + 4, TX + 6, TY - 1, first_col)
    shift_high = shifted(1, TY - 1, TX + 3, TX + 5, TX + 7, 0, last_col)
    above = jnp.where(gx == 0, 0.0, 1.0)
    below = jnp.where(gx == n_gx - 1, 0.0, 1.0)

    def frame(a):
        for d in range(8):
            halo(a, d).wait_recv()
        whole = src[a].reshape(source_rows, WIDE)
        cat[a, :, 0:WIDE] = dot(shift_low, whole).astype(BF16)
        cat[a, :, 2 * WIDE : 3 * WIDE] = dot(shift_high, whole).astype(BF16)
        cat[a, 0:TY, WIDE : 2 * WIDE] = (src[a, 0].astype(F32) * above).astype(BF16)
        cat[a, TY : TY + CELLS, WIDE : 2 * WIDE] = src[a, 1 : TX + 1].reshape(CELLS, WIDE)
        cat[a, TY + CELLS :, WIDE : 2 * WIDE] = (src[a, TX + 1].astype(F32) * below).astype(BF16)

    def rows_of(a, dx):
        return cat[a, dx * TY : dx * TY + CELLS, :]

    def convolve(a, layer):
        return sum(dot(rows_of(a, dx), band[layer, dx], NT) for dx in range(3))

    sample = samples_ref[...]
    sample_cell = jnp.broadcast_to(lax.div(sample, NZ).astype(F32), (256, 256)).T
    sample_level = jnp.broadcast_to(lax.rem(sample, NZ).astype(F32), (256, 256)).T
    lane = iota((256, 256), 1)
    gather = jnp.where(sample_cell == lane.astype(F32), 1.0, 0.0).astype(BF16)
    level = jnp.where(sample_level == lax.div(lane, C).astype(F32), 1.0, 0.0)
    low_lanes = iota((64, 128), 1) < 64

    frame(FIELD)
    hidden_pre = convolve(FIELD, 0)
    sigma = 1.0 / (1.0 + jnp.exp(-hidden_pre))
    keep(HIDDEN, (hidden_pre * sigma).astype(BF16))
    for d in range(8):
        halo(HIDDEN, d).start()

    frame(COT)
    back = jnp.zeros((CELLS, WIDE), F32)
    for dx in range(3):
        for dy in range(3):
            back += dot(
                cat[COT, dx * TY : dx * TY + CELLS, dy * WIDE : (dy + 1) * WIDE],
                band[1, 2 - dx, :, (2 - dy) * WIDE : (3 - dy) * WIDE],
            )
    delta = (back * sigma * (1.0 + hidden_pre * (1.0 - sigma))).astype(BF16)

    hidden = src[HIDDEN, 1 : TX + 1].reshape(CELLS, WIDE)
    delta_t = delta.astype(F32).T.astype(BF16)
    hidden_t = hidden.astype(F32).T.astype(BF16)
    for dx in range(3):
        grads[0, dx] = dot(delta_t, rows_of(FIELD, dx))
        grads[1, dx] = dot(hidden_t, rows_of(COT, dx))

    chunk = HALF // ring

    def place(k, value):
        half, rest = divmod(k * 64, HALF)
        at, row = divmod(rest, chunk)
        pay[half, at, row : row + 64, :] = value

    count = float(n_gx * n_gy * 256)
    scale = 1.0 / jnp.sqrt(jnp.float32(n_gx * n_gy * CELLS * NZ))

    def gram(values):
        picked = dot(gather, values) * level
        full_gram = dot(picked.T.astype(BF16), picked.astype(BF16))
        even = full_gram[0:64, 0:128] + full_gram[128:192, 128:256]
        odd = full_gram[64:128, 0:128] + full_gram[192:256, 128:256]
        return even, odd

    def two_grams(one, two):
        even, odd = gram(one)
        even2, odd2 = gram(two)
        return jnp.where(low_lanes, even + swap_halves(odd), swap_halves(even2) + odd2) / count

    field = src[FIELD, 1 : TX + 1].reshape(CELLS, WIDE)
    cot = src[COT, 1 : TX + 1].reshape(CELLS, WIDE)
    place(27, two_grams(field, cot))
    place(28, two_grams(hidden, delta))
    for k in range(29, BLOCKS):
        place(k, jnp.zeros((64, 128), F32))

    def pieces(layer, dx, dy):
        def piece(a, h):
            at = dy * WIDE + h * 128
            return grads[layer, dx, a * 64 : (a + 1) * 64, at : at + 128]

        return piece(0, 0) + piece(2, 1), piece(1, 0) + piece(3, 1), piece(2, 0), piece(1, 1)

    for dx in range(3):
        for dy in range(3):
            even, odd, before, after = pieces(0, dx, dy)
            even2, odd2, before2, after2 = pieces(1, 2 - dx, 2 - dy)
            swapped_even, swapped_odd = swap_halves(even), swap_halves(odd)
            swapped_even2, swapped_odd2 = swap_halves(even2), swap_halves(odd2)
            k = (dx * 3 + dy) * 3
            one = (odd + swap_halves(before), even + swapped_odd, after + swapped_even)
            two = (swap_halves(after2) + even2, swapped_even2 + odd2, swapped_odd2 + before2)
            for dz in range(3):
                place(k + dz, jnp.where(low_lanes, one[dz], two[dz]) * scale)

    def to_core(j):
        return copy(pay.at[1 - core, j], core_in.at[j], core_send.at[j], core_recv.at[j], partner)

    def to_ring(j):
        return copy(
            pay.at[core, j], axis_in.at[rank], axis_send.at[j], axis_recv.at[rank], on_ring(j)
        )

    def from_ring(j):
        return copy(pay.at[core, j], axis_in.at[j], axis_send.at[j], axis_recv.at[j], on_ring(j))

    def to_plane(j):
        return copy(
            plane_out.at[lax.rem(j, part)],
            plane_in.at[spot],
            plane_send.at[j],
            plane_recv.at[spot],
            on_plane(j),
        )

    def from_plane(j):
        return copy(
            plane_out.at[lax.rem(j, part)],
            plane_in.at[j],
            plane_send.at[j],
            plane_recv.at[j],
            on_plane(j),
        )

    def to_group(j):
        mine = full.at[core, rank, slot]
        return copy(
            mine, mine, gather_send.at[j], gather_recv.at[slot], on_plane(group * part + j)
        )

    def from_group(j):
        theirs = full.at[core, rank, j]
        return copy(
            theirs, theirs, gather_send.at[j], gather_recv.at[j], on_plane(group * part + j)
        )

    def spread(j):
        mine = full.at[core, rank]
        return copy(mine, mine, spread_send.at[j], spread_recv.at[rank], on_ring(j))

    def from_spread(j):
        theirs = full.at[core, j]
        return copy(theirs, theirs, spread_send.at[j], spread_recv.at[j], on_ring(j))

    def to_back(j):
        mine = full.at[core, j]
        return copy(mine, mine, back_send.at[j], back_recv.at[j], partner)

    def from_back(j):
        theirs = full.at[1 - core, j]
        return copy(theirs, theirs, back_send.at[j], back_recv.at[j], partner)

    partner_rank = z + core * (y - z)

    @pl.loop(1, ring + 1)
    def _(k):
        to_core(lax.rem(partner_rank + k, ring)).start()

    @pl.loop(1, ring)
    def _(k):
        j = lax.rem(rank + k, ring)
        to_core(j).wait_recv()
        pay[core, j] = pay[core, j] + core_in[j]
        to_ring(j).start()

    to_core(rank).wait_recv()
    axis_in[rank] = pay[core, rank] + core_in[rank]

    frame(HIDDEN)
    output = (field.astype(F32) + convolve(HIDDEN, 1)).astype(BF16).astype(F32)
    for b in range(4):
        block = output[b * 64 : (b + 1) * 64]
        stacked = jnp.concatenate([block[:, j * 64 : (j + 1) * 64] for j in range(NZ)], axis=0)
        out_ref[b * 256 : (b + 1) * 256, :] = dot(to_cells, stacked.astype(BF16)).astype(BF16)

    @pl.loop(1, ring)
    def _(k):
        from_ring(lax.rem(rank + ring - k, ring)).wait_recv()

    total = axis_in[0]
    for j in range(1, ring):
        total += axis_in[j]
    plane_out[...] = total.reshape(part, chunk // part, 128)

    @pl.loop(1, plane)
    def _(k):
        to_plane(lax.rem(spot + k, plane)).start()

    plane_in[spot] = plane_out[slot]

    @pl.loop(1, plane)
    def _(k):
        from_plane(lax.rem(spot + plane - k, plane)).wait_recv()

    full[core, rank, slot] = jnp.sum(plane_in[...], axis=0)

    @pl.loop(1, part)
    def _(k):
        to_group(lax.rem(slot + k, part)).start()

    @pl.loop(1, part)
    def _(k):
        from_group(lax.rem(slot + part - k, part)).wait_recv()

    @pl.loop(1, ring)
    def _(k):
        spread(lax.rem(rank + k, ring)).start()

    to_back(rank).start()

    @pl.loop(1, ring)
    def _(k):
        j = lax.rem(rank + ring - k, ring)
        from_spread(j).wait_recv()
        to_back(j).start()

    @pl.loop(0, ring)
    def _(j):
        from_back(j).wait_recv()

    def summed(k, n):
        half, rest = divmod(k * 64, HALF)
        at, row = divmod(rest, chunk)
        if n * 64 <= chunk - row:
            step = chunk // part
            if row % step == 0 and (n * 64) % step == 0:
                return full[half, at, row // step : (row + n * 64) // step].reshape(n * 64, 128)
        if n == 1:
            step = chunk // part
            return full[half, at, row // step, row % step : row % step + 64]
        return jnp.concatenate([summed(k + m, 1) for m in range(n)], axis=0)

    metric[...] = jnp.zeros((256, 256), F32)
    for m in range(4):
        lanes = slice((m // 2) * 128, (m // 2 + 1) * 128)
        block = summed(27 + m // 2, 1)
        mine = low_lanes if m % 2 == 0 else jnp.logical_not(low_lanes)
        metric[m * 64 : (m + 1) * 64, lanes] = jnp.where(mine, block, 0.0)
    eye = jnp.where(iota((256, 256), 0) == lane, 1.0, 0.0)
    matrix = metric[...] + 0.1 * eye
    norms = [
        jnp.sqrt(jnp.sum(matrix[m * 64 : (m + 1) * 64] * matrix[m * 64 : (m + 1) * 64]))
        for m in range(4)
    ]
    approx = jnp.concatenate([eye[m * 64 : (m + 1) * 64] / norms[m] for m in range(4)], axis=0)
    for _ in range(NS_ITERS):
        approx = dot32(approx, 2.0 * eye - dot32(matrix, approx))
    corner = approx[0:128, 0:128]
    right_second = jnp.where(low_lanes, 0.0, approx[64:128, 0:128])
    left_second = approx[128:192, 128:256]
    right_first = swap_halves(approx[192:256, 128:256])

    def four(block):
        low = jnp.where(low_lanes, block, 0.0)
        high = jnp.where(low_lanes, 0.0, swap_halves(block))
        none = jnp.zeros((64, 128), F32)
        return jnp.concatenate(
            [
                jnp.concatenate([low, none], axis=1),
                jnp.concatenate([high, none], axis=1),
                jnp.concatenate([none, low], axis=1),
                jnp.concatenate([none, high], axis=1),
            ],
            axis=0,
        )

    right_four = four(right_first)
    left_four = four(left_second)
    for q in range(7):
        block = summed(4 * q, 4)
        done = dot32(right_four, dot32(block, corner))
        lanes = jnp.concatenate([done[m * 64 : (m + 1) * 64, 0:64] for m in range(4)], axis=1)
        other = dot32(dot32(right_second, block, NT), left_four)
        width = 256 if q < 6 else 192
        first_out[:, q * 256 : q * 256 + width] = lanes[:, 0:width]
        second_out[:, q * 256 : q * 256 + width] = other[:, 0:width]

    for a in range(3):
        for d in range(8):
            halo(a, d).wait_send()

    @pl.loop(0, ring)
    def _(j):
        to_core(j).wait_send()
        to_back(j).wait_send()

    @pl.loop(1, ring)
    def _(k):
        j = lax.rem(rank + k, ring)
        to_ring(j).wait_send()
        spread(j).wait_send()

    @pl.loop(1, plane)
    def _(k):
        to_plane(lax.rem(spot + k, plane)).wait_send()

    @pl.loop(1, part)
    def _(k):
        to_group(lax.rem(slot + k, part)).wait_send()


def solution(mesh):
    n_gx, n_gy = mesh.shape["gx"], mesh.shape["gy"]
    ring = n_gx // 4
    z_hi = ring // 2
    plane = (n_gy // z_hi) * ring
    part = plane // 2
    chunk = HALF // ring
    vmem = pl.BlockSpec(memory_space=pltpu.VMEM)
    dma = pltpu.SemaphoreType.DMA

    def local(field, first_kernel, second_kernel, cotangent, samples):
        cells = field.shape[0] * field.shape[1] * field.shape[2]
        output, first, second = pl.pallas_call(
            functools.partial(kernel, (n_gx, n_gy, z_hi, ring, plane, part)),
            out_shape=(
                jax.ShapeDtypeStruct((cells, C), BF16),
                jax.ShapeDtypeStruct((C, 27 * C), F32),
                jax.ShapeDtypeStruct((C, 27 * C), F32),
            ),
            in_specs=[vmem] * 5,
            out_specs=(vmem,) * 3,
            scratch_shapes=[
                pltpu.VMEM((3, TX + 8, TY, WIDE), BF16),
                pltpu.VMEM((3, 2, TX, WIDE), BF16),
                pltpu.VMEM((3, (TX + 2) * TY, 3 * WIDE), BF16),
                pltpu.VMEM((2, 3, WIDE, 3 * WIDE), BF16),
                pltpu.VMEM((2, 3, WIDE, 3 * WIDE), F32),
                pltpu.VMEM((2, ring, chunk, 128), F32),
                pltpu.VMEM((ring, chunk, 128), F32),
                pltpu.VMEM((ring, chunk, 128), F32),
                pltpu.VMEM((part, chunk // part, 128), F32),
                pltpu.VMEM((plane, chunk // part, 128), F32),
                pltpu.VMEM((2, ring, part, chunk // part, 128), F32),
                pltpu.VMEM((256, 256), F32),
                dma((3, 8)),
                dma((3, 8)),
                dma((ring,)),
                dma((ring,)),
                dma((ring,)),
                dma((ring,)),
                dma((plane,)),
                dma((plane,)),
                dma((part,)),
                dma((part,)),
                dma((ring,)),
                dma((ring,)),
                dma((ring,)),
                dma((ring,)),
            ],
            compiler_params=pltpu.CompilerParams(
                collective_id=0, has_side_effects=True, vmem_limit_bytes=48 * 1024 * 1024
            ),
        )(
            field.reshape(cells, C),
            first_kernel.T,
            second_kernel.T,
            cotangent.reshape(cells, C),
            samples.reshape(1, -1),
        )
        return output.reshape(field.shape), first.T, second.T

    placed = (P("gx", "gy", None, None), P(), P(), P("gx", "gy", None, None), P("gx", "gy", None))
    return jax.shard_map(
        local,
        mesh=mesh,
        in_specs=placed,
        out_specs=(P("gx", "gy", None, None), P(), P()),
        check_vma=False,
    )
```

time: 845 us -> 78.1 us (0.09)
  waiting for transfers between devices: 455 us -> 0 us
  local copies, waits for them, and re-layouts: 165 us -> 6.69 us
  loops' own time: 95.5 us -> 0 us
  Pallas kernels: 0 us -> 70.5 us
  matrix products: 51.6 us -> 0 us
  starting transfers between devices: 42.1 us -> 0 us
  between operations: 17.7 us -> 0.65 us
  other arithmetic: 9.56 us -> 0 us
    psum x2 -> x0, waiting for transfers between devices: 453 us -> none  [the longest x1 261 us: local(): lax.psum((second_grad, first_grad), ('gx', 'gy'))]
    another operation x5 -> x0, loops' own time: 95.5 us -> none  [the longest x3 94.1 us: convolve(): result = lax.map(one_row, jnp.arange(xlen, dtype=jnp.int32))]
    pallas_call x0 -> x1, Pallas kernels: none -> 70.5 us  [local(): pl.pallas_call(functools.partial(kernel, (n_gx, n_gy, z_hi, ring, plane,...]
    slice x85 -> x0, local copies, waits for them, and re-layouts: 70.3 us -> none  [the longest x80 68.1 us: patches(): slab[first, second:second + ylen, third:third + zlen, :]]
    dot_general x128 -> x0, matrix products: 51.6 us -> none  [the longest x48 19.9 us: one_row(): jnp.dot(patches(padded, row_index, ylen, zlen), kernel, preferred_element...]
    ppermute x12 -> x0, starting transfers between devices: 41.8 us -> none  [the longest x6 28.9 us: with_halo(): lax.ppermute(lax.slice_in_dim(block, block.shape[dim] - width, None, axis...]
    concatenate x82 -> x0, local copies, waits for them, and re-layouts: 41.5 us -> none  [the longest x80 41.4 us: patches(): return jnp.concatenate(pieces, -1).reshape(ylen * zlen, -1)]
    dynamic_slice x48 -> x0, local copies, waits for them, and re-layouts: 38.6 us -> none  [convolve(): result = lax.map(one_row, jnp.arange(xlen, dtype=jnp.int32))]
  transfers between devices with their start and end apart: 14 -> 0, of which waited for: 3 -> 0; matrix products, arithmetic and copies ran while one was open for 17% -> 0% of each run, Pallas kernels for 0% -> 0%
where the time goes in v1:
time: 78.1 us; the launch traced here: 77.8 us
  Pallas kernels  70.5 us (90%)
  local copies, waits for them, and re-layouts  6.69 us (9%)
    pallas_call x1, Pallas kernels, local(): pl.pallas_call(functools.partial(kernel, (n_gx, n_gy, z_hi, ring, plane,...  70.5 us
    unnamed x13, local copies, waits for them, and re-layouts  6.69 us

profile of v1, /device:TPU:1, one launch (start us, length us, event | category | flops | bytes accessed | tf_op | source)
XLA Modules:
  0.0 77.8 jit_solution(5819899710444075962)
XLA Ops:
  0.6 0.0 copy-start.4
  0.6 0.7 copy-done.4
  1.3 0.0 copy-start
  1.3 0.9 %copy-done = bf16[16,16,4,64]{3,2,1,0:T(4,128)(2,1)S(1)} copy-done((bf16[16,16,4,64]{3,2,1,0:T(4,128)(2,1)S(1)}, bf16[16,16,4,64]{3,2,1,0:T(4,128)(2,1)}, u32[]{:S(2)}) %copy-start) | copy-done | bytes 131096
  2.3 0.0 copy-start.1
  2.3 0.9 %copy-done.1 = bf16[16,16,4,64]{3,2,1,0:T(4,128)(2,1)S(1)} copy-done((bf16[16,16,4,64]{3,2,1,0:T(4,128)(2,1)S(1)}, bf16[16,16,4,64]{3,2,1,0:T(4,128)(2,1)}, u32[]{:S(2)}) %copy-start.1) | copy-done | bytes 131096
  3.2 0.0 copy-start.2
  3.2 0.9 %copy-done.2 = bf16[1728,64]{0,1:T(8,128)(2,1)S(1)} copy-done((bf16[1728,64]{0,1:T(8,128)(2,1)S(1)}, bf16[1728,64]{0,1:T(8,128)(2,1)}, u32[]{:S(2)}) %copy-start.2) | copy-done | bytes 221208
  4.2 0.0 copy-start.3
  4.2 0.9 %copy-done.3 = bf16[1728,64]{0,1:T(8,128)(2,1)S(1)} copy-done((bf16[1728,64]{0,1:T(8,128)(2,1)S(1)}, bf16[1728,64]{0,1:T(8,128)(2,1)}, u32[]{:S(2)}) %copy-start.3) | copy-done | bytes 221208
  5.1 70.5 %shard_map.76 = (bf16[1024,64]{1,0:T(8,128)(2,1)S(1)}, f32[64,1728]{1,0:T(8,128)S(1)}, f32[64,1728]{1,0:T(8,128)S(1)}) custom-call(bf16[1024,64]{1,0:T(8,128)(2,1)S(1)} %bitcast.10, bf16[64,1728]{1,0:T(8,128)(2,1)S(1)} %bitcast.13, bf16[64,1728]{1,0:T(8,128)(2,1)S(1)} %bitcast.14, bf16[1024,64]{1,0:T(8,128)(2,1)S(1)} %bitcast.11, s32[1,256]{1,0:T(1,128)S(1)} %bitcast.15), custom_call_target="tpu_custom_call" | custom-call | tf_op jit(solution)/shard_map/pallas_call | solution.py:535
  75.6 0.7 copy.11
  76.3 0.8 copy.12
  77.0 0.8 copy.13
Async XLA Ops:
  0.6 0.7 copy-start.4
  1.3 0.9 %copy-start = (bf16[16,16,4,64]{3,2,1,0:T(4,128)(2,1)S(1)}, bf16[16,16,4,64]{3,2,1,0:T(4,128)(2,1)}, u32[]{:S(2)}) copy-start(bf16[16,16,4,64]{3,2,1,0:T(4,128)(2,1)} %param.5) | copy-start | bytes 393220
  2.3 0.9 %copy-start.1 = (bf16[16,16,4,64]{3,2,1,0:T(4,128)(2,1)S(1)}, bf16[16,16,4,64]{3,2,1,0:T(4,128)(2,1)}, u32[]{:S(2)}) copy-start(bf16[16,16,4,64]{3,2,1,0:T(4,128)(2,1)} %param.8) | copy-start | bytes 393220
  3.2 0.9 %copy-start.2 = (bf16[1728,64]{0,1:T(8,128)(2,1)S(1)}, bf16[1728,64]{0,1:T(8,128)(2,1)}, u32[]{:S(2)}) copy-start(bf16[1728,64]{0,1:T(8,128)(2,1)} %param.6) | copy-start | bytes 663556
  4.2 0.9 %copy-start.3 = (bf16[1728,64]{0,1:T(8,128)(2,1)S(1)}, bf16[1728,64]{0,1:T(8,128)(2,1)}, u32[]{:S(2)}) copy-start(bf16[1728,64]{0,1:T(8,128)(2,1)} %param.7) | copy-start | bytes 663556

commit v2 on v1

v2 whole, which is shorter than its diff:
```python
import functools

import jax
import jax.numpy as jnp
from jax import lax
from jax.experimental import pallas as pl
from jax.experimental.pallas import tpu as pltpu
from jax.sharding import PartitionSpec as P

MESH = pl.DeviceIdType.MESH
F32 = jnp.float32
BF16 = jnp.bfloat16
NS_ITERS = 5
C = 64
TX = 16
TY = 16
NZ = 4
WIDE = NZ * C
CELLS = TX * TY
BLOCKS = 32
HALF = BLOCKS * 64 // 2
FIELD, COT, HIDDEN = 0, 1, 2
NN = (((1,), (0,)), ((), ()))
NT = (((1,), (1,)), ((), ()))


def dot(a, b, dims=NN):
    return lax.dot_general(a, b, dims, preferred_element_type=F32)


def split(value):
    high = value.astype(BF16)
    return high, (value - high.astype(F32)).astype(BF16)


def dot3(a, b):
    return dot(jnp.concatenate([a[0], a[0], a[1]], axis=1), jnp.concatenate([b[0], b[1], b[0]], axis=0))


def dot3_t(a, b):
    return dot(
        jnp.concatenate([a[0], a[0], a[1]], axis=1), jnp.concatenate([b[0], b[1], b[0]], axis=1), NT
    )


def iota(shape, dim):
    return lax.broadcasted_iota(jnp.int32, shape, dim)


def onehot(target, shape):
    return jnp.where(iota(shape, 1) == target, 1.0, 0.0).astype(BF16)


def swap_halves(value):
    return pltpu.roll(value, 64, 1)


def by_distance(count):
    return sorted(range(1, count), key=lambda k: -min(k, count - k))


def kernel(
    sizes,
    field_hbm,
    first_hbm,
    second_hbm,
    cot_hbm,
    samples_hbm,
    out_ref,
    first_out,
    second_out,
    field_ref,
    first_ref,
    second_ref,
    cot_ref,
    samples_ref,
    src,
    col,
    cat,
    band,
    grads,
    pay,
    core_in,
    one_in,
    two_out,
    two_in,
    x_in,
    whole,
    result,
    gram_pay,
    gram_core,
    gram_one,
    gram_two,
    gram_x,
    gram_all,
    metric,
    load_sem,
    halo_send,
    halo_recv,
    send_sems,
    recv_sems,
):
    n_gx, n_gy, z_hi, ring, n_x = sizes
    gx = lax.axis_index("gx")
    gy = lax.axis_index("gy")
    core = lax.rem(gx, 2)
    z_low = lax.rem(lax.div(gx, 2), 2)
    y = lax.div(gx, 4)
    x = lax.div(gy, z_hi)
    z = lax.rem(gy, z_hi) * 2 + z_low

    def load(k, source, target):
        return pltpu.make_async_copy(source, target, load_sem.at[k])

    loads = [
        load(k, *pair)
        for k, pair in enumerate(
            (
                (field_hbm, field_ref),
                (cot_hbm, cot_ref),
                (first_hbm, first_ref),
                (second_hbm, second_ref),
                (samples_hbm, samples_ref),
            )
        )
    ]
    for one in loads:
        one.start()

    rank = y + core * (z - y)
    rank_two = z + core * (y - z)
    partner = (gx + 1 - 2 * core, gy)

    def along_y(j):
        return gx + 4 * (j - y), gy

    def along_z(j):
        return gx + 2 * (lax.rem(j, 2) - z_low), x * z_hi + lax.div(j, 2)

    def on_ring(j):
        (ax, ay), (bx, by) = along_y(j), along_z(j)
        return (ax + core * (bx - ax), ay + core * (by - ay))

    def on_ring_two(j):
        (bx, by), (ax, ay) = along_y(j), along_z(j)
        return (ax + core * (bx - ax), ay + core * (by - ay))

    def along_x(j):
        return (gx, gy + z_hi * (j - x))

    def neighbour(dx, dy):
        return (lax.rem(gx + n_gx + dx, n_gx), lax.rem(gy + n_gy + dy, n_gy))

    barrier = pltpu.get_barrier_semaphore()

    def signal(where):
        pl.semaphore_signal(barrier, inc=1, device_id=where, device_id_type=MESH)

    sides = ((1, 0), (-1, 0), (0, 1), (0, -1), (1, 1), (1, -1), (-1, 1), (-1, -1))
    for side in sides:
        signal(neighbour(*side))
    signal(partner)
    for k in by_distance(ring):
        signal(on_ring(lax.rem(rank + k, ring)))
        signal(on_ring_two(lax.rem(rank_two + k, ring)))
    for k in range(1, n_x):
        signal(along_x(lax.rem(x + k, n_x)))

    def copy(source, target, send, recv, where):
        return pltpu.make_async_remote_copy(
            src_ref=source,
            dst_ref=target,
            send_sem=send,
            recv_sem=recv,
            device_id=where,
            device_id_type=MESH,
        )

    def halo(a, d):
        side = sides[d]
        if side[0] == 0:
            source = col.at[a, 1 if side[1] > 0 else 0]
        else:
            source = src.at[a, TX if side[0] > 0 else 1]
        landing = (0, TX + 1, TX + 2, TX + 3, TX + 4, TX + 5, TX + 6, TX + 7)[d]
        return copy(
            source, src.at[a, landing], halo_send.at[a, d], halo_recv.at[a, d], neighbour(*side)
        )

    class Exchange:
        def __init__(self, stage, count, me, where, source, target):
            self.stage, self.count, self.me, self.where = stage, count, me, where
            self.source, self.target = source, target
            self.order = by_distance(count)

        def outgoing(self, k):
            j = lax.rem(self.me + k, self.count)
            return copy(
                self.source(j),
                self.target(self.me),
                send_sems.at[self.stage, k],
                recv_sems.at[self.stage, k],
                self.where(j),
            )

        def sender(self, k):
            return lax.rem(self.me + self.count - k, self.count)

        def start(self):
            for k in self.order:
                self.outgoing(k).start()

        def arrived(self, k):
            there = self.target(self.sender(k))
            copy(
                there, there, send_sems.at[self.stage, k], recv_sems.at[self.stage, k], partner
            ).wait_recv()

        def wait(self):
            for k in reversed(self.order):
                self.arrived(k)

        def settle(self):
            for k in self.order:
                self.outgoing(k).wait_send()

    def to_core(layer, k):
        j = lax.rem(rank_two + k, ring)
        return copy(
            pay.at[layer, 1 - core, j],
            core_in.at[layer, j],
            send_sems.at[12 * layer, k],
            recv_sems.at[12 * layer, k],
            partner,
        )

    def from_core(layer, k):
        j = lax.rem(rank + k, ring)
        return copy(
            pay.at[layer, core, j],
            core_in.at[layer, j],
            send_sems.at[12 * layer, k],
            recv_sems.at[12 * layer, k],
            partner,
        )

    def to_back(k):
        there = result.at[core, lax.rem(rank + ring - k, ring)]
        return copy(there, there, send_sems.at[1, k], recv_sems.at[1, k], partner)

    def from_back(k):
        there = result.at[1 - core, lax.rem(rank_two + ring - k, ring)]
        return copy(there, there, send_sems.at[1, k], recv_sems.at[1, k], partner)

    ones = [
        Exchange(
            stage,
            ring,
            rank,
            on_ring,
            functools.partial(lambda layer, j: pay.at[layer, core, j], layer),
            functools.partial(lambda layer, j: one_in.at[layer, j], layer),
        )
        for layer, stage in enumerate((2, 13))
    ]
    two = Exchange(3, ring, rank_two, on_ring_two, lambda j: two_out.at[j], lambda j: two_in.at[j])
    third = Exchange(4, n_x, x, along_x, lambda j: x_in.at[x], lambda j: x_in.at[j])
    gather_two = Exchange(
        5, ring, rank_two, on_ring_two, lambda j: whole.at[rank_two], lambda j: whole.at[j]
    )
    spread = Exchange(
        6, ring, rank, on_ring, lambda j: result.at[core, rank], lambda j: result.at[core, j]
    )
    gram_to_core = copy(
        gram_pay.at[1 - core], gram_core, send_sems.at[7, 0], recv_sems.at[7, 0], partner
    )
    gram_first = Exchange(
        8, ring, rank, on_ring, lambda j: gram_pay.at[core, j], lambda j: gram_one.at[j]
    )
    gram_second = Exchange(
        9, ring, rank_two, on_ring_two, lambda j: gram_two.at[rank_two], lambda j: gram_two.at[j]
    )
    gram_third = Exchange(10, n_x, x, along_x, lambda j: gram_x.at[x], lambda j: gram_x.at[j])
    gram_gather = Exchange(
        11, ring, rank, on_ring, lambda j: gram_all.at[core, rank], lambda j: gram_all.at[core, j]
    )
    gram_back = copy(
        gram_all.at[core], gram_all.at[core], send_sems.at[7, 1], recv_sems.at[7, 1], partner
    )
    gram_from_back = copy(
        gram_all.at[1 - core], gram_all.at[1 - core], send_sems.at[7, 1], recv_sems.at[7, 1], partner
    )

    edge_rows = iota((2 * TX, 1), 0)
    edges = onehot(jnp.where(edge_rows < TX, edge_rows * TY, (edge_rows - TX) * TY + TY - 1), (2 * TX, CELLS))

    def keep(a, value):
        src[a, 1 : TX + 1] = value.reshape(TX, TY, WIDE)
        col[a] = dot(edges, value).astype(BF16).reshape(2, TX, WIDE)

    rows256 = iota((256, 1), 0)
    to_columns = onehot(lax.rem(rows256, 64) * NZ + lax.div(rows256, 64), (256, 256))
    to_cells = onehot(lax.rem(rows256, NZ) * 64 + lax.div(rows256, NZ), (256, 256))

    def columns_of(ref):
        out = []
        for b in range(4):
            moved = dot(to_columns, ref[b * 256 : (b + 1) * 256, :])
            out.append(jnp.concatenate([moved[i * 64 : (i + 1) * 64] for i in range(NZ)], axis=1))
        return jnp.concatenate(out, axis=0).astype(BF16)

    loads[0].wait()
    keep(FIELD, columns_of(field_ref))
    loads[1].wait()
    keep(COT, columns_of(cot_ref))
    pl.semaphore_wait(barrier, len(sides) + 1 + 2 * (ring - 1) + n_x - 1)
    for d in range(8):
        halo(FIELD, d).start()
    for d in range(8):
        halo(COT, d).start()

    def build_band(layer, ref):
        nothing = jnp.zeros((64, 64), F32)
        for k in range(9):
            low, mid, high = (
                ref[:, (3 * k + i) * 64 : (3 * k + i + 1) * 64].astype(F32) for i in range(3)
            )
            lanes = slice((k % 3) * WIDE, (k % 3 + 1) * WIDE)
            for out_z, parts in enumerate(
                (
                    (mid, high, nothing, nothing),
                    (low, mid, high, nothing),
                    (nothing, low, mid, high),
                    (nothing, nothing, low, mid),
                )
            ):
                band[layer, k // 3, out_z * 64 : (out_z + 1) * 64, lanes] = jnp.concatenate(
                    parts, axis=1
                ).astype(BF16)

    loads[2].wait()
    build_band(0, first_ref)
    loads[3].wait()
    build_band(1, second_ref)
    loads[4].wait()
    framed_rows = (TX + 2) * TY
    source_rows = (TX + 8) * TY
    i = iota((framed_rows, 1), 0)
    r = lax.div(i, TY)
    c = lax.rem(i, TY)
    first_row, last_row = jnp.where(gx == 0, 0, -1), jnp.where(gx == n_gx - 1, TX + 1, -1)
    first_col, last_col = jnp.where(gy == 0, 0, -1), jnp.where(gy == n_gy - 1, TY - 1, -1)
    outside = (r == first_row) | (r == last_row)

    def shifted(step, at, column_slot, low_slot, high_slot, pick, outer):
        edge = jnp.where(
            r == 0,
            low_slot * TY + pick,
            jnp.where(r == TX + 1, high_slot * TY + pick, column_slot * TY + r - 1),
        )
        target = jnp.where(c == at, edge, i + step)
        return onehot(jnp.where(outside | (c == outer), -1, target), (framed_rows, source_rows))

    shift_low = shifted(-1, 0, TX + 2, TX + 4, TX + 6, TY - 1, first_col)
    shift_high = shifted(1, TY - 1, TX + 3, TX + 5, TX + 7, 0, last_col)
    above = jnp.where(gx == 0, 0.0, 1.0)
    below = jnp.where(gx == n_gx - 1, 0.0, 1.0)

    def frame(a):
        for d in range(8):
            halo(a, d).wait_recv()
        whole = src[a].reshape(source_rows, WIDE)
        cat[a, :, 0:WIDE] = dot(shift_low, whole).astype(BF16)
        cat[a, :, 2 * WIDE : 3 * WIDE] = dot(shift_high, whole).astype(BF16)
        cat[a, 0:TY, WIDE : 2 * WIDE] = (src[a, 0].astype(F32) * above).astype(BF16)
        cat[a, TY : TY + CELLS, WIDE : 2 * WIDE] = src[a, 1 : TX + 1].reshape(CELLS, WIDE)
        cat[a, TY + CELLS :, WIDE : 2 * WIDE] = (src[a, TX + 1].astype(F32) * below).astype(BF16)

    def rows_of(a, dx):
        return cat[a, dx * TY : dx * TY + CELLS, :]

    def convolve(a, layer):
        return sum(dot(rows_of(a, dx), band[layer, dx], NT) for dx in range(3))

    sample = samples_ref[...]
    sample_cell = jnp.broadcast_to(lax.div(sample, NZ).astype(F32), (256, 256)).T
    sample_level = jnp.broadcast_to(lax.rem(sample, NZ).astype(F32), (256, 256)).T
    lane = iota((256, 256), 1)
    gather = jnp.where(sample_cell == lane.astype(F32), 1.0, 0.0).astype(BF16)
    level = jnp.where(sample_level == lax.div(lane, C).astype(F32), 1.0, 0.0)
    low_lanes = iota((64, 128), 1) < 64

    def gram(values):
        picked = dot(gather, values) * level
        full_gram = dot(picked.T.astype(BF16), picked.astype(BF16))
        even = full_gram[0:64, 0:128] + full_gram[128:192, 128:256]
        odd = full_gram[64:128, 0:128] + full_gram[192:256, 128:256]
        return even, odd

    count = float(n_gx * n_gy * 256)
    scale = 1.0 / jnp.sqrt(jnp.float32(n_gx * n_gy * CELLS * NZ))
    gram_rows = 64 // ring

    def two_grams(one, two):
        even, odd = gram(one)
        even2, odd2 = gram(two)
        both = jnp.where(low_lanes, even + swap_halves(odd), swap_halves(even2) + odd2)
        return (both / count).reshape(ring, gram_rows, 128)

    field = src[FIELD, 1 : TX + 1].reshape(CELLS, WIDE)
    cot = src[COT, 1 : TX + 1].reshape(CELLS, WIDE)
    gram_pay[0] = two_grams(field, cot)

    chunk = HALF // ring

    def assemble(layer, flip):
        taps = [None] * 27
        for dx in range(3):
            for dy in range(3):

                def piece(a, h):
                    at = dy * WIDE + h * 128
                    return grads[layer, dx, a * 64 : (a + 1) * 64, at : at + 128]

                even, odd = piece(0, 0) + piece(2, 1), piece(1, 0) + piece(3, 1)
                pairs = ((odd, piece(2, 0)), (even, odd), (piece(1, 1), even))
                for e in range(3):
                    tap = (dx * 3 + dy) * 3 + e
                    taps[26 - tap if flip else tap] = pairs[e]
        for k in range(BLOCKS // 2):
            low, high = 2 * k, 2 * k + 1
            value = jnp.zeros((64, 128), F32)
            if low < 27:
                value = jnp.where(low_lanes, taps[low][0] + swap_halves(taps[low][1]), 0.0) * scale
            if high < 27:
                other = (swap_halves(taps[high][0]) + taps[high][1]) * scale
                value = jnp.where(low_lanes, value, other)
            per = chunk // 128
            half, rest = divmod(k, ring * per)
            at, p = divmod(rest, per)
            pay[layer, half, at, p * 64 : (p + 1) * 64, :] = value

    def send_on(layer):
        for k in ones[layer].order:
            from_core(layer, k).wait_recv()
            j = lax.rem(rank + k, ring)
            pay[layer, core, j] = pay[layer, core, j] + core_in[layer, j]
            ones[layer].outgoing(k).start()
        from_core(layer, 0).wait_recv()
        one_in[layer, rank] = pay[layer, core, rank] + core_in[layer, rank]

    frame(FIELD)
    hidden_pre = convolve(FIELD, 0)
    sigma = 1.0 / (1.0 + jnp.exp(-hidden_pre))
    hidden = (hidden_pre * sigma).astype(BF16)
    keep(HIDDEN, hidden)
    for d in range(8):
        halo(HIDDEN, d).start()

    frame(COT)
    hidden_t = hidden.astype(F32).T.astype(BF16)
    for dx in range(3):
        grads[1, dx] = dot(hidden_t, rows_of(COT, dx))
    assemble(1, True)
    for k in ones[1].order + [0]:
        to_core(1, k).start()

    back = jnp.zeros((CELLS, WIDE), F32)
    for dx in range(3):
        for dy in range(3):
            back += dot(
                cat[COT, dx * TY : dx * TY + CELLS, dy * WIDE : (dy + 1) * WIDE],
                band[1, 2 - dx, :, (2 - dy) * WIDE : (3 - dy) * WIDE],
            )
    delta = (back * sigma * (1.0 + hidden_pre * (1.0 - sigma))).astype(BF16)
    gram_pay[1] = two_grams(hidden, delta)
    gram_to_core.start()
    send_on(1)

    delta_t = delta.astype(F32).T.astype(BF16)
    for dx in range(3):
        grads[0, dx] = dot(delta_t, rows_of(FIELD, dx))
    gram_to_core.wait_recv()
    gram_pay[core] = gram_pay[core] + gram_core[...]
    gram_one[rank] = gram_pay[core, rank]
    gram_first.start()
    assemble(0, False)
    for k in ones[0].order + [0]:
        to_core(0, k).start()
    send_on(0)

    gram_first.wait()
    gram_two[rank_two] = jnp.sum(gram_one[...], axis=0)
    gram_second.start()

    frame(HIDDEN)
    output = (field.astype(F32) + convolve(HIDDEN, 1)).astype(BF16).astype(F32)
    for b in range(4):
        block = output[b * 64 : (b + 1) * 64]
        stacked = jnp.concatenate([block[:, j * 64 : (j + 1) * 64] for j in range(NZ)], axis=0)
        out_ref[b * 256 : (b + 1) * 256, :] = dot(to_cells, stacked.astype(BF16)).astype(BF16)

    gram_second.wait()
    gram_x[x] = jnp.sum(gram_two[...], axis=0)
    gram_third.start()

    part = chunk // 2 // ring
    for layer in range(2):
        ones[layer].wait()
        total = one_in[layer, 0]
        for j in range(1, ring):
            total += one_in[layer, j]
        two_out[:, layer * part : (layer + 1) * part] = total.reshape(ring, part, 128)
    two_in[rank_two] = two_out[rank_two]
    two.start()
    for a in range(3):
        for d in range(8):
            halo(a, d).wait_send()

    gram_third.wait()
    gram_all[core, rank] = jnp.sum(gram_x[...], axis=0)
    gram_gather.start()
    gram_to_core.wait_send()
    for k in range(ring):
        to_core(1, k).wait_send()
        to_core(0, k).wait_send()

    two.wait()
    x_in[x] = jnp.sum(two_in[...], axis=0)
    third.start()
    for stage in (ones[1], ones[0], gram_first):
        stage.settle()
    gram_gather.wait()
    gram_back.start()

    third.wait()
    whole[rank_two] = jnp.sum(x_in[...], axis=0)
    gather_two.start()

    gram_from_back.wait_recv()
    metric[...] = jnp.zeros((256, 256), F32)
    for m in range(4):
        lanes = slice((m // 2) * 128, (m // 2 + 1) * 128)
        mine = low_lanes if m % 2 == 0 else jnp.logical_not(low_lanes)
        block = gram_all[m // 2].reshape(64, 128)
        metric[m * 64 : (m + 1) * 64, lanes] = jnp.where(mine, block, 0.0)
    eye = jnp.where(iota((256, 256), 0) == lane, 1.0, 0.0)
    matrix = metric[...] + 0.1 * eye
    norms = [
        jnp.sqrt(jnp.sum(matrix[m * 64 : (m + 1) * 64] * matrix[m * 64 : (m + 1) * 64]))
        for m in range(4)
    ]
    approx = jnp.concatenate([eye[m * 64 : (m + 1) * 64] / norms[m] for m in range(4)], axis=0)
    matrix = split(matrix)

    def refine(value):
        parts = split(value)
        return dot3(parts, split(2.0 * eye - dot3(matrix, parts)))

    for _ in range(NS_ITERS):
        approx = refine(approx)

    def twice(block, low):
        other = swap_halves(block)
        first, second = (block, other) if low else (other, block)
        return split(
            jnp.concatenate(
                [jnp.where(low_lanes, first, 0.0), jnp.where(low_lanes, 0.0, second)], axis=0
            )
        )

    left_first = twice(approx[0:64, 0:128], True)
    right_second = twice(approx[64:128, 0:128], False)
    none = jnp.zeros((64, 128), F32)
    left_second = split(
        jnp.concatenate([jnp.where(low_lanes, approx[128:192, 128:256], 0.0), none], axis=0)
    )
    right_first = split(
        jnp.where(low_lanes, swap_halves(approx[192:256, 128:256]), 0.0)
    )

    for stage in (two, third, gram_second, gram_third, gram_gather):
        stage.settle()
    gram_back.wait_send()
    gather_two.wait()
    pairs = chunk // 128
    both = [
        whole[:, layer * part : (layer + 1) * part].reshape(pairs, 64, 128) for layer in range(2)
    ]
    for p in range(pairs):
        block = split(jnp.concatenate([both[0][p], none], axis=0))
        result[core, rank, p, 0:64, :] = dot3(
            right_first, split(dot3(block, left_first))
        ).astype(BF16)
        block = split(jnp.concatenate([both[1][p], none], axis=0))
        done = dot3(split(dot3_t(right_second, block)), left_second)
        result[core, rank, p, 64:128, :] = jnp.where(
            low_lanes, done[0:64], swap_halves(done[64:128])
        ).astype(BF16)
    spread.start()
    to_back(0).start()
    for k in reversed(spread.order):
        spread.arrived(k)
        to_back(k).start()
    for k in [0] + spread.order[::-1]:
        from_back(k).wait_recv()

    for k in range(14):
        half, rest = divmod(k, HALF // 128)
        at, p = divmod(rest, pairs)
        lanes = 128 if k < 13 else 64
        first_out[:, k * 128 : k * 128 + lanes] = result[half, at, p, 0:64, 0:lanes]
        second_out[:, k * 128 : k * 128 + lanes] = result[half, at, p, 64:128, 0:lanes]

    for k in range(ring):
        to_back(k).wait_send()
    gather_two.settle()
    spread.settle()


def solution(mesh):
    n_gx, n_gy = mesh.shape["gx"], mesh.shape["gy"]
    ring = n_gx // 4
    z_hi = ring // 2
    n_x = n_gy // z_hi
    chunk = HALF // ring
    most = max(ring, n_x)
    vmem = pl.BlockSpec(memory_space=pltpu.VMEM)
    anywhere = pl.BlockSpec(memory_space=pl.ANY)
    dma = pltpu.SemaphoreType.DMA

    def local(field, first_kernel, second_kernel, cotangent, samples):
        cells = field.shape[0] * field.shape[1] * field.shape[2]
        output, first, second = pl.pallas_call(
            functools.partial(kernel, (n_gx, n_gy, z_hi, ring, n_x)),
            out_shape=(
                jax.ShapeDtypeStruct((cells, C), BF16),
                jax.ShapeDtypeStruct((C, 27 * C), BF16),
                jax.ShapeDtypeStruct((C, 27 * C), BF16),
            ),
            in_specs=[anywhere] * 5,
            out_specs=(vmem,) * 3,
            scratch_shapes=[
                pltpu.VMEM((cells, C), BF16),
                pltpu.VMEM((C, 27 * C), BF16),
                pltpu.VMEM((C, 27 * C), BF16),
                pltpu.VMEM((cells, C), BF16),
                pltpu.VMEM((1, 256), jnp.int32),
                pltpu.VMEM((3, TX + 8, TY, WIDE), BF16),
                pltpu.VMEM((3, 2, TX, WIDE), BF16),
                pltpu.VMEM((3, (TX + 2) * TY, 3 * WIDE), BF16),
                pltpu.VMEM((2, 3, WIDE, 3 * WIDE), BF16),
                pltpu.VMEM((2, 3, WIDE, 3 * WIDE), F32),
                pltpu.VMEM((2, 2, ring, chunk // 2, 128), F32),
                pltpu.VMEM((2, ring, chunk // 2, 128), F32),
                pltpu.VMEM((2, ring, chunk // 2, 128), F32),
                pltpu.VMEM((ring, chunk // ring, 128), F32),
                pltpu.VMEM((ring, chunk // ring, 128), F32),
                pltpu.VMEM((n_x, chunk // ring, 128), F32),
                pltpu.VMEM((ring, chunk // ring, 128), F32),
                pltpu.VMEM((2, ring, chunk // 128, 128, 128), BF16),
                pltpu.VMEM((2, ring, 64 // ring, 128), F32),
                pltpu.VMEM((ring, 64 // ring, 128), F32),
                pltpu.VMEM((ring, 64 // ring, 128), F32),
                pltpu.VMEM((ring, 64 // ring, 128), F32),
                pltpu.VMEM((n_x, 64 // ring, 128), F32),
                pltpu.VMEM((2, ring, 64 // ring, 128), F32),
                pltpu.VMEM((256, 256), F32),
                dma((5,)),
                dma((3, 8)),
                dma((3, 8)),
                dma((14, most)),
                dma((14, most)),
            ],
            compiler_params=pltpu.CompilerParams(
                collective_id=0, has_side_effects=True, vmem_limit_bytes=54 * 1024 * 1024
            ),
        )(
            field.reshape(cells, C),
            first_kernel.T,
            second_kernel.T,
            cotangent.reshape(cells, C),
            samples.reshape(1, -1),
        )
        return output.reshape(field.shape), first.astype(F32).T, second.astype(F32).T

    placed = (P("gx", "gy", None, None), P(), P(), P("gx", "gy", None, None), P("gx", "gy", None))
    return jax.shard_map(
        local,
        mesh=mesh,
        in_specs=placed,
        out_specs=(P("gx", "gy", None, None), P(), P()),
        check_vma=False,
    )
```

time: 78.1 us -> 64.4 us (0.82)
  Pallas kernels: 70.5 us -> 60.9 us
  local copies, waits for them, and re-layouts: 6.69 us -> 0.71 us
  other arithmetic: 0 us -> 2.07 us
    pallas_call x1, Pallas kernels: 70.5 us -> 60.9 us  [local(): pl.pallas_call(functools.partial(kernel, (n_gx, n_gy, z_hi, ring, n_x)),...]
    unnamed x13 -> x3, local copies, waits for them, and re-layouts: 6.69 us -> 0.71 us
    transpose x0 -> x1, other arithmetic: none -> 2.07 us  [local(): second.astype(F32)]
where the time goes in v2:
time: 64.4 us; the launch traced here: 64.3 us
  Pallas kernels  60.9 us (95%)
  other arithmetic  2.07 us (3%)
  local copies, waits for them, and re-layouts  0.71 us (1%)
  between operations  0.65 us (1%)
    pallas_call x1, Pallas kernels, local(): pl.pallas_call(functools.partial(kernel, (n_gx, n_gy, z_hi, ring, n_x)),...  60.9 us
    transpose x1, other arithmetic, local(): second.astype(F32)  2.07 us

profile of v2, /device:TPU:1, one launch (start us, length us, event | category | flops | bytes accessed | tf_op | source)
XLA Modules:
  0.0 64.3 jit_solution(15077609526226841126)
XLA Ops:
  0.6 60.9 %shard_map.76 = (bf16[1024,64]{1,0:T(8,128)(2,1)}, bf16[64,1728]{1,0:T(8,128)(2,1)}, bf16[64,1728]{1,0:T(8,128)(2,1)}) custom-call(bf16[1024,64]{1,0:T(8,128)(2,1)} %bitcast.10, bf16[64,1728]{1,0:T(8,128)(2,1)} %bitcast.13, bf16[64,1728]{1,0:T(8,128)(2,1)} %bitcast.14, bf16[1024,64]{1,0:T(8,128)(2,1)} %bitcast.11, s32[1,256]{1,0:T(1,128)} %bitcast.15), custom_call_target="tpu_custom_call" | custom-call | tf_op jit(solution)/shard_map/pallas_call | solution.py:634
  61.5 0.0 copy-start
  61.5 2.1 %convert_bitcast_fusion = (f32[1728,64]{0,1:T(8,128)}, f32[1728,64]{0,1:T(8,128)}) fusion(bf16[64,1728]{1,0:T(8,128)(2,1)} %get-tuple-element.8, bf16[64,1728]{1,0:T(8,128)(2,1)} %get-tuple-element.7), kind=kLoop, calls=%fused_computation | loop fusion | flops 221184 | bytes 1327104 | tf_op jit(solution)/shard_map/transpose | solution.py:685
  63.6 0.0 copy-done
  63.6 0.7 %copy.9 = bf16[16,16,4,64]{3,2,1,0:T(4,128)(2,1)} copy(bf16[16,16,4,64]{3,2,1,0:T(4,128)(2,1)S(1)} %bitcast.12) | data formatting | bytes 262144
Async XLA Ops:
  61.5 2.1 %copy-start = (bf16[1024,64]{1,0:T(8,128)(2,1)S(1)}, bf16[1024,64]{1,0:T(8,128)(2,1)}, u32[]{:S(2)}) copy-start(bf16[1024,64]{1,0:T(8,128)(2,1)} %get-tuple-element.6) | copy-start | bytes 393220

commit v3 on v2

--- a/solution.py
+++ b/solution.py
@@ -66,7 +66,7 @@
     second_hbm,
     cot_hbm,
     samples_hbm,
-    out_ref,
+    out_hbm,
     first_out,
     second_out,
     field_ref,
@@ -74,6 +74,7 @@
     second_ref,
     cot_ref,
     samples_ref,
+    out_ref,
     src,
     col,
     cat,
@@ -88,13 +89,13 @@
     whole,
     result,
     gram_pay,
-    gram_core,
     gram_one,
     gram_two,
     gram_x,
     gram_all,
     metric,
     load_sem,
+    store_sem,
     halo_send,
     halo_recv,
     send_sems,
@@ -148,6 +149,11 @@
     def along_x(j):
         return (gx, gy + z_hi * (j - x))
 
+    seat = x * 2 + core
+
+    def along_seats(j):
+        return (gx + lax.rem(j, 2) - core, gy + z_hi * (lax.div(j, 2) - x))
+
     def neighbour(dx, dy):
         return (lax.rem(gx + n_gx + dx, n_gx), lax.rem(gy + n_gy + dy, n_gy))
 
@@ -159,12 +165,11 @@
     sides = ((1, 0), (-1, 0), (0, 1), (0, -1), (1, 1), (1, -1), (-1, 1), (-1, -1))
     for side in sides:
         signal(neighbour(*side))
-    signal(partner)
     for k in by_distance(ring):
         signal(on_ring(lax.rem(rank + k, ring)))
         signal(on_ring_two(lax.rem(rank_two + k, ring)))
-    for k in range(1, n_x):
-        signal(along_x(lax.rem(x + k, n_x)))
+    for k in range(1, 2 * n_x):
+        signal(along_seats(lax.rem(seat + k, 2 * n_x)))
 
     def copy(source, target, send, recv, where):
         return pltpu.make_async_remote_copy(
@@ -271,24 +276,17 @@
     spread = Exchange(
         6, ring, rank, on_ring, lambda j: result.at[core, rank], lambda j: result.at[core, j]
     )
-    gram_to_core = copy(
-        gram_pay.at[1 - core], gram_core, send_sems.at[7, 0], recv_sems.at[7, 0], partner
-    )
     gram_first = Exchange(
-        8, ring, rank, on_ring, lambda j: gram_pay.at[core, j], lambda j: gram_one.at[j]
+        8, ring, y, along_y, lambda j: gram_pay.at[j], lambda j: gram_one.at[j]
     )
     gram_second = Exchange(
-        9, ring, rank_two, on_ring_two, lambda j: gram_two.at[rank_two], lambda j: gram_two.at[j]
-    )
-    gram_third = Exchange(10, n_x, x, along_x, lambda j: gram_x.at[x], lambda j: gram_x.at[j])
+        9, ring, z, along_z, lambda j: gram_two.at[z], lambda j: gram_two.at[j]
+    )
+    gram_third = Exchange(
+        10, 2 * n_x, seat, along_seats, lambda j: gram_x.at[seat], lambda j: gram_x.at[j]
+    )
     gram_gather = Exchange(
-        11, ring, rank, on_ring, lambda j: gram_all.at[core, rank], lambda j: gram_all.at[core, j]
-    )
-    gram_back = copy(
-        gram_all.at[core], gram_all.at[core], send_sems.at[7, 1], recv_sems.at[7, 1], partner
-    )
-    gram_from_back = copy(
-        gram_all.at[1 - core], gram_all.at[1 - core], send_sems.at[7, 1], recv_sems.at[7, 1], partner
+        11, ring, y, along_y, lambda j: gram_all.at[y], lambda j: gram_all.at[j]
     )
 
     edge_rows = iota((2 * TX, 1), 0)
@@ -313,7 +311,7 @@
     keep(FIELD, columns_of(field_ref))
     loads[1].wait()
     keep(COT, columns_of(cot_ref))
-    pl.semaphore_wait(barrier, len(sides) + 1 + 2 * (ring - 1) + n_x - 1)
+    pl.semaphore_wait(barrier, len(sides) + 2 * (ring - 1) + 2 * n_x - 1)
     for d in range(8):
         halo(FIELD, d).start()
     for d in range(8):
@@ -399,17 +397,16 @@
 
     count = float(n_gx * n_gy * 256)
     scale = 1.0 / jnp.sqrt(jnp.float32(n_gx * n_gy * CELLS * NZ))
-    gram_rows = 64 // ring
 
     def two_grams(one, two):
         even, odd = gram(one)
         even2, odd2 = gram(two)
         both = jnp.where(low_lanes, even + swap_halves(odd), swap_halves(even2) + odd2)
-        return (both / count).reshape(ring, gram_rows, 128)
+        return (both / count).reshape(ring // 2, 128 // ring, 128)
 
     field = src[FIELD, 1 : TX + 1].reshape(CELLS, WIDE)
     cot = src[COT, 1 : TX + 1].reshape(CELLS, WIDE)
-    gram_pay[0] = two_grams(field, cot)
+    gram_pay[: ring // 2] = two_grams(field, cot)
 
     chunk = HALF // ring
 
@@ -473,24 +470,21 @@
                 band[1, 2 - dx, :, (2 - dy) * WIDE : (3 - dy) * WIDE],
             )
     delta = (back * sigma * (1.0 + hidden_pre * (1.0 - sigma))).astype(BF16)
-    gram_pay[1] = two_grams(hidden, delta)
-    gram_to_core.start()
+    gram_pay[ring // 2 :] = two_grams(hidden, delta)
+    gram_first.start()
+    gram_one[y] = gram_pay[y]
     send_on(1)
 
     delta_t = delta.astype(F32).T.astype(BF16)
     for dx in range(3):
         grads[0, dx] = dot(delta_t, rows_of(FIELD, dx))
-    gram_to_core.wait_recv()
-    gram_pay[core] = gram_pay[core] + gram_core[...]
-    gram_one[rank] = gram_pay[core, rank]
-    gram_first.start()
     assemble(0, False)
     for k in ones[0].order + [0]:
         to_core(0, k).start()
     send_on(0)
 
     gram_first.wait()
-    gram_two[rank_two] = jnp.sum(gram_one[...], axis=0)
+    gram_two[z] = jnp.sum(gram_one[...], axis=0)
     gram_second.start()
 
     frame(HIDDEN)
@@ -499,9 +493,11 @@
         block = output[b * 64 : (b + 1) * 64]
         stacked = jnp.concatenate([block[:, j * 64 : (j + 1) * 64] for j in range(NZ)], axis=0)
         out_ref[b * 256 : (b + 1) * 256, :] = dot(to_cells, stacked.astype(BF16)).astype(BF16)
+    store_out = pltpu.make_async_copy(out_ref, out_hbm, store_sem.at[0])
+    store_out.start()
 
     gram_second.wait()
-    gram_x[x] = jnp.sum(gram_two[...], axis=0)
+    gram_x[seat] = jnp.sum(gram_two[...], axis=0)
     gram_third.start()
 
     part = chunk // 2 // ring
@@ -518,9 +514,8 @@
             halo(a, d).wait_send()
 
     gram_third.wait()
-    gram_all[core, rank] = jnp.sum(gram_x[...], axis=0)
+    gram_all[y] = jnp.sum(gram_x[...], axis=0)
     gram_gather.start()
-    gram_to_core.wait_send()
     for k in range(ring):
         to_core(1, k).wait_send()
         to_core(0, k).wait_send()
@@ -530,19 +525,18 @@
     third.start()
     for stage in (ones[1], ones[0], gram_first):
         stage.settle()
-    gram_gather.wait()
-    gram_back.start()
-
     third.wait()
     whole[rank_two] = jnp.sum(x_in[...], axis=0)
     gather_two.start()
 
-    gram_from_back.wait_recv()
+    gram_gather.wait()
+
+    grams = gram_all[...].reshape(2, 64, 128)
     metric[...] = jnp.zeros((256, 256), F32)
     for m in range(4):
         lanes = slice((m // 2) * 128, (m // 2 + 1) * 128)
         mine = low_lanes if m % 2 == 0 else jnp.logical_not(low_lanes)
-        block = gram_all[m // 2].reshape(64, 128)
+        block = grams[m // 2]
         metric[m * 64 : (m + 1) * 64, lanes] = jnp.where(mine, block, 0.0)
     eye = jnp.where(iota((256, 256), 0) == lane, 1.0, 0.0)
     matrix = metric[...] + 0.1 * eye
@@ -550,15 +544,21 @@
         jnp.sqrt(jnp.sum(matrix[m * 64 : (m + 1) * 64] * matrix[m * 64 : (m + 1) * 64]))
         for m in range(4)
     ]
-    approx = jnp.concatenate([eye[m * 64 : (m + 1) * 64] / norms[m] for m in range(4)], axis=0)
-    matrix = split(matrix)
-
-    def refine(value):
-        parts = split(value)
-        return dot3(parts, split(2.0 * eye - dot3(matrix, parts)))
-
-    for _ in range(NS_ITERS):
-        approx = refine(approx)
+    error = eye - jnp.concatenate(
+        [matrix[m * 64 : (m + 1) * 64] / norms[m] for m in range(4)], axis=0
+    )
+    factor = eye + error
+    parts = split(error)
+    error = dot3(parts, parts)
+    for step in range(1, NS_ITERS):
+        parts = split(error)
+        if step < NS_ITERS - 1:
+            both = tuple(jnp.concatenate([f, e], axis=0) for f, e in zip(split(factor), parts))
+            moved = dot3(both, parts)
+            factor, error = factor + moved[0:256], moved[256:512]
+        else:
+            factor = factor + dot3(split(factor), parts)
+    approx = jnp.concatenate([factor[m * 64 : (m + 1) * 64] / norms[m] for m in range(4)], axis=0)
 
     def twice(block, low):
         other = swap_halves(block)
@@ -581,7 +581,6 @@
 
     for stage in (two, third, gram_second, gram_third, gram_gather):
         stage.settle()
-    gram_back.wait_send()
     gather_two.wait()
     pairs = chunk // 128
     both = [
@@ -616,6 +615,7 @@
         to_back(k).wait_send()
     gather_two.settle()
     spread.settle()
+    store_out.wait()
 
 
 def solution(mesh):
@@ -624,7 +624,7 @@
     z_hi = ring // 2
     n_x = n_gy // z_hi
     chunk = HALF // ring
-    most = max(ring, n_x)
+    most = max(ring, 2 * n_x)
     vmem = pl.BlockSpec(memory_space=pltpu.VMEM)
     anywhere = pl.BlockSpec(memory_space=pl.ANY)
     dma = pltpu.SemaphoreType.DMA
@@ -639,13 +639,14 @@
                 jax.ShapeDtypeStruct((C, 27 * C), BF16),
             ),
             in_specs=[anywhere] * 5,
-            out_specs=(vmem,) * 3,
+            out_specs=(anywhere, vmem, vmem),
             scratch_shapes=[
                 pltpu.VMEM((cells, C), BF16),
                 pltpu.VMEM((C, 27 * C), BF16),
                 pltpu.VMEM((C, 27 * C), BF16),
                 pltpu.VMEM((cells, C), BF16),
                 pltpu.VMEM((1, 256), jnp.int32),
+                pltpu.VMEM((cells, C), BF16),
                 pltpu.VMEM((3, TX + 8, TY, WIDE), BF16),
                 pltpu.VMEM((3, 2, TX, WIDE), BF16),
                 pltpu.VMEM((3, (TX + 2) * TY, 3 * WIDE), BF16),
@@ -659,14 +660,14 @@
                 pltpu.VMEM((n_x, chunk // ring, 128), F32),
                 pltpu.VMEM((ring, chunk // ring, 128), F32),
                 pltpu.VMEM((2, ring, chunk // 128, 128, 128), BF16),
-                pltpu.VMEM((2, ring, 64 // ring, 128), F32),
-                pltpu.VMEM((ring, 64 // ring, 128), F32),
-                pltpu.VMEM((ring, 64 // ring, 128), F32),
-                pltpu.VMEM((ring, 64 // ring, 128), F32),
-                pltpu.VMEM((n_x, 64 // ring, 128), F32),
-                pltpu.VMEM((2, ring, 64 // ring, 128), F32),
+                pltpu.VMEM((ring, 128 // ring, 128), F32),
+                pltpu.VMEM((ring, 128 // ring, 128), F32),
+                pltpu.VMEM((ring, 128 // ring, 128), F32),
+                pltpu.VMEM((2 * n_x, 128 // ring, 128), F32),
+                pltpu.VMEM((ring, 128 // ring, 128), F32),
                 pltpu.VMEM((256, 256), F32),
                 dma((5,)),
+                dma((1,)),
                 dma((3, 8)),
                 dma((3, 8)),
                 dma((14, most)),

time: 64.4 us -> 62.4 us (0.969)
  Pallas kernels: 60.9 us -> 58.9 us
    pallas_call x1, Pallas kernels: 60.9 us -> 58.9 us  [local(): pl.pallas_call(functools.partial(kernel, (n_gx, n_gy, z_hi, ring, n_x)),...]
where the time goes in v3:
time: 62.4 us; the launch traced here: 62.3 us
  Pallas kernels  58.9 us (94%)
  other arithmetic  2.07 us (3%)
  local copies, waits for them, and re-layouts  0.71 us (1%)
  between operations  0.65 us (1%)
    pallas_call x1, Pallas kernels, local(): pl.pallas_call(functools.partial(kernel, (n_gx, n_gy, z_hi, ring, n_x)),...  58.9 us
    transpose x1, other arithmetic, local(): second.astype(F32)  2.07 us

profile of v3, /device:TPU:1, one launch (start us, length us, event | category | flops | bytes accessed | tf_op | source)
XLA Modules:
  0.0 62.3 jit_solution(14853199567425149625)
XLA Ops:
  0.6 58.9 %shard_map.76 = (bf16[1024,64]{1,0:T(8,128)(2,1)}, bf16[64,1728]{1,0:T(8,128)(2,1)}, bf16[64,1728]{1,0:T(8,128)(2,1)}) custom-call(bf16[1024,64]{1,0:T(8,128)(2,1)} %bitcast.10, bf16[64,1728]{1,0:T(8,128)(2,1)} %bitcast.13, bf16[64,1728]{1,0:T(8,128)(2,1)} %bitcast.14, bf16[1024,64]{1,0:T(8,128)(2,1)} %bitcast.11, s32[1,256]{1,0:T(1,128)} %bitcast.15), custom_call_target="tpu_custom_call" | custom-call | tf_op jit(solution)/shard_map/pallas_call | solution.py:634
  59.5 0.0 copy-start
  59.5 2.1 %convert_bitcast_fusion = (f32[1728,64]{0,1:T(8,128)}, f32[1728,64]{0,1:T(8,128)}) fusion(bf16[64,1728]{1,0:T(8,128)(2,1)} %get-tuple-element.8, bf16[64,1728]{1,0:T(8,128)(2,1)} %get-tuple-element.7), kind=kLoop, calls=%fused_computation | loop fusion | flops 221184 | bytes 1327104 | tf_op jit(solution)/shard_map/transpose | solution.py:686
  61.6 0.0 copy-done
  61.6 0.7 %copy.9 = bf16[16,16,4,64]{3,2,1,0:T(4,128)(2,1)} copy(bf16[16,16,4,64]{3,2,1,0:T(4,128)(2,1)S(1)} %bitcast.12) | data formatting | bytes 262144
Async XLA Ops:
  59.5 2.1 %copy-start = (bf16[1024,64]{1,0:T(8,128)(2,1)S(1)}, bf16[1024,64]{1,0:T(8,128)(2,1)}, u32[]{:S(2)}) copy-start(bf16[1024,64]{1,0:T(8,128)(2,1)} %get-tuple-element.6) | copy-start | bytes 393220

commit v4 on v3

--- a/solution.py
+++ b/solution.py
@@ -674,7 +674,7 @@
                 dma((14, most)),
             ],
             compiler_params=pltpu.CompilerParams(
-                collective_id=0, has_side_effects=True, vmem_limit_bytes=54 * 1024 * 1024
+                collective_id=0, has_side_effects=True, vmem_limit_bytes=(53 * 1024 + 360) * 1024
             ),
         )(
             field.reshape(cells, C),

time: 62.4 us -> 61.3 us (0.982)
  other arithmetic: 2.07 us -> 0.98 us
  Pallas kernels: 58.9 us -> 58.1 us
  local copies, waits for them, and re-layouts: 0.71 us -> 1.38 us
    transpose x1, other arithmetic: 2.07 us -> 0.98 us  [local(): second.astype(F32)]
    pallas_call x1, Pallas kernels: 58.9 us -> 58.1 us  [local(): pl.pallas_call(functools.partial(kernel, (n_gx, n_gy, z_hi, ring, n_x)),...]
    unnamed x3 -> x5, local copies, waits for them, and re-layouts: 0.71 us -> 1.38 us
where the time goes in v4:
time: 61.3 us; the launch traced here: 61.1 us
  Pallas kernels  58.1 us (95%)
  local copies, waits for them, and re-layouts  1.38 us (2%)
  other arithmetic  0.98 us (2%)
  between operations  0.66 us (1%)
    pallas_call x1, Pallas kernels, local(): pl.pallas_call(functools.partial(kernel, (n_gx, n_gy, z_hi, ring, n_x)),...  58.1 us
    unnamed x5, local copies, waits for them, and re-layouts  1.38 us

profile of v4, /device:TPU:1, one launch (start us, length us, event | category | flops | bytes accessed | tf_op | source)
XLA Modules:
  0.0 61.1 jit_solution(17433750108230660860)
XLA Ops:
  0.6 0.0 copy-start
  0.6 0.7 %copy-done = s32[1,1,256]{2,1,0:T(1,128)S(1)} copy-done((s32[1,1,256]{2,1,0:T(1,128)S(1)}, s32[1,1,256]{2,1,0:T(1,128)}, u32[]{:S(2)}) %copy-start) | copy-done | bytes 1048
  1.3 58.1 %shard_map.76 = (bf16[1024,64]{1,0:T(8,128)(2,1)}, bf16[64,1728]{1,0:T(8,128)(2,1)S(1)}, bf16[64,1728]{1,0:T(8,128)(2,1)S(1)}) custom-call(bf16[1024,64]{1,0:T(8,128)(2,1)} %bitcast.11, bf16[64,1728]{1,0:T(8,128)(2,1)} %bitcast.14, bf16[64,1728]{1,0:T(8,128)(2,1)} %bitcast.15, bf16[1024,64]{1,0:T(8,128)(2,1)} %bitcast.12, s32[1,256]{1,0:T(1,128)S(1)} %bitcast.10), custom_call_target="tpu_custom_call" | custom-call | tf_op jit(solution)/shard_map/pallas_call | solution.py:634
  59.4 0.0 copy-start.1
  59.4 1.0 %convert_bitcast_fusion = (f32[1728,64]{0,1:T(8,128)}, f32[1728,64]{0,1:T(8,128)}) fusion(bf16[64,1728]{1,0:T(8,128)(2,1)S(1)} %get-tuple-element.8, bf16[64,1728]{1,0:T(8,128)(2,1)S(1)} %get-tuple-element.7), kind=kLoop, calls=%fused_computation | loop fusion | flops 221184 | bytes 1327104 | tf_op jit(solution)/shard_map/transpose | solution.py:686
  60.4 0.0 copy-done.1
  60.4 0.7 %copy.9 = bf16[16,16,4,64]{3,2,1,0:T(4,128)(2,1)} copy(bf16[16,16,4,64]{3,2,1,0:T(4,128)(2,1)S(1)} %bitcast.13) | data formatting | bytes 262144
Async XLA Ops:
  0.6 0.7 %copy-start = (s32[1,1,256]{2,1,0:T(1,128)S(1)}, s32[1,1,256]{2,1,0:T(1,128)}, u32[]{:S(2)}) copy-start(s32[1,1,256]{2,1,0:T(1,128)} %param.9) | copy-start | bytes 3076
  59.4 1.0 %copy-start.1 = (bf16[1024,64]{1,0:T(8,128)(2,1)S(1)}, bf16[1024,64]{1,0:T(8,128)(2,1)}, u32[]{:S(2)}) copy-start(bf16[1024,64]{1,0:T(8,128)(2,1)} %get-tuple-element.6) | copy-start | bytes 393220

commit v5 on v4

--- a/solution.py
+++ b/solution.py
@@ -496,10 +496,6 @@
     store_out = pltpu.make_async_copy(out_ref, out_hbm, store_sem.at[0])
     store_out.start()
 
-    gram_second.wait()
-    gram_x[seat] = jnp.sum(gram_two[...], axis=0)
-    gram_third.start()
-
     part = chunk // 2 // ring
     for layer in range(2):
         ones[layer].wait()
@@ -512,6 +508,10 @@
     for a in range(3):
         for d in range(8):
             halo(a, d).wait_send()
+
+    gram_second.wait()
+    gram_x[seat] = jnp.sum(gram_two[...], axis=0)
+    gram_third.start()
 
     gram_third.wait()
     gram_all[y] = jnp.sum(gram_x[...], axis=0)
@@ -597,10 +597,12 @@
             low_lanes, done[0:64], swap_halves(done[64:128])
         ).astype(BF16)
     spread.start()
+    gather_two.settle()
     to_back(0).start()
     for k in reversed(spread.order):
         spread.arrived(k)
         to_back(k).start()
+    spread.settle()
     for k in [0] + spread.order[::-1]:
         from_back(k).wait_recv()
 
@@ -613,8 +615,6 @@
 
     for k in range(ring):
         to_back(k).wait_send()
-    gather_two.settle()
-    spread.settle()
     store_out.wait()
 
 

time: 61.3 us -> 59.9 us (0.977)
  Pallas kernels: 58.1 us -> 56.7 us
    pallas_call x1, Pallas kernels: 58.1 us -> 56.7 us  [local(): pl.pallas_call(functools.partial(kernel, (n_gx, n_gy, z_hi, ring, n_x)),...]
where the time goes in v5:
time: 59.9 us; the launch traced here: 59.8 us
  Pallas kernels  56.7 us (95%)
  local copies, waits for them, and re-layouts  1.38 us (2%)
  other arithmetic  0.98 us (2%)
  between operations  0.66 us (1%)
    pallas_call x1, Pallas kernels, local(): pl.pallas_call(functools.partial(kernel, (n_gx, n_gy, z_hi, ring, n_x)),...  56.7 us
    unnamed x5, local copies, waits for them, and re-layouts  1.38 us

profile of v5, /device:TPU:1, one launch (start us, length us, event | category | flops | bytes accessed | tf_op | source)
XLA Modules:
  0.0 59.8 jit_solution(9397435452037024222)
XLA Ops:
  0.6 0.0 copy-start
  0.6 0.7 %copy-done = s32[1,1,256]{2,1,0:T(1,128)S(1)} copy-done((s32[1,1,256]{2,1,0:T(1,128)S(1)}, s32[1,1,256]{2,1,0:T(1,128)}, u32[]{:S(2)}) %copy-start) | copy-done | bytes 1048
  1.3 56.7 %shard_map.76 = (bf16[1024,64]{1,0:T(8,128)(2,1)}, bf16[64,1728]{1,0:T(8,128)(2,1)S(1)}, bf16[64,1728]{1,0:T(8,128)(2,1)S(1)}) custom-call(bf16[1024,64]{1,0:T(8,128)(2,1)} %bitcast.11, bf16[64,1728]{1,0:T(8,128)(2,1)} %bitcast.14, bf16[64,1728]{1,0:T(8,128)(2,1)} %bitcast.15, bf16[1024,64]{1,0:T(8,128)(2,1)} %bitcast.12, s32[1,256]{1,0:T(1,128)S(1)} %bitcast.10), custom_call_target="tpu_custom_call" | custom-call | tf_op jit(solution)/shard_map/pallas_call | solution.py:634
  58.1 0.0 copy-start.1
  58.1 1.0 %convert_bitcast_fusion = (f32[1728,64]{0,1:T(8,128)}, f32[1728,64]{0,1:T(8,128)}) fusion(bf16[64,1728]{1,0:T(8,128)(2,1)S(1)} %get-tuple-element.8, bf16[64,1728]{1,0:T(8,128)(2,1)S(1)} %get-tuple-element.7), kind=kLoop, calls=%fused_computation | loop fusion | flops 221184 | bytes 1327104 | tf_op jit(solution)/shard_map/transpose | solution.py:686
  59.1 0.0 copy-done.1
  59.1 0.7 %copy.9 = bf16[16,16,4,64]{3,2,1,0:T(4,128)(2,1)} copy(bf16[16,16,4,64]{3,2,1,0:T(4,128)(2,1)S(1)} %bitcast.13) | data formatting | bytes 262144
Async XLA Ops:
  0.6 0.7 %copy-start = (s32[1,1,256]{2,1,0:T(1,128)S(1)}, s32[1,1,256]{2,1,0:T(1,128)}, u32[]{:S(2)}) copy-start(s32[1,1,256]{2,1,0:T(1,128)} %param.9) | copy-start | bytes 3076
  58.1 1.0 %copy-start.1 = (bf16[1024,64]{1,0:T(8,128)(2,1)S(1)}, bf16[1024,64]{1,0:T(8,128)(2,1)}, u32[]{:S(2)}) copy-start(bf16[1024,64]{1,0:T(8,128)(2,1)} %get-tuple-element.6) | copy-start | bytes 393220
